TPU v7x, 256 devices: a whole 4x4x8 slice. The times are simulated.
256 devices in a mesh: dp: 32 (over y, z), seq: 8 (over x, core).
Axes of the slice: x: 4, y: 4, z: 8, core: 2. Of those that a mesh axis runs over, the one named last changes fastest.
Arguments:
- q_in: bfloat16 [32768, 3072], P(('dp', 'seq')), may hold values from -6 to 6
- k_in: bfloat16 [32768, 3072], P(('dp', 'seq')), may hold values from -6 to 6
- v_in: bfloat16 [32768, 3072], P(('dp', 'seq')), may hold values from -6 to 6
- q_gain: float32 [128], replicated, may hold values from 0.6 to 5
- k_gain: float32 [128], replicated, may hold values from 0.6 to 5
- image_tokens: int32 [64], replicated, may hold values from 192 to 576, as said below
- text_tokens: int32 [64], replicated, may hold values from 1 to 128
Outputs:
- attended: bfloat16 [32768, 3072], P(('dp', 'seq'))
Inputs may be any that keep to these rules, and one draw needn't show every extreme that they name: The samples fill the pack exactly: the image_tokens sum to 24576.
All inputs are finite; a program needn't handle non-finite values.
Results may differ from a plain program's by a relative error of at most 0.012.
The roundings to bfloat16 on the way count: a program that leaves them out, or rounds other values in their place, can miss the bound.
Values may be sent and summed in bfloat16 or wider, within the bound.
A program may use at most 64 MiB of HBM per device.

v0:
```python
import jax
import jax.numpy as jnp
from jax import lax
from jax.sharding import PartitionSpec as P

HD = 128
TXT = 128


EPS = 1e-06


def with_halo(cells, sides, width):
    for axis, dim in sides:
        count = lax.axis_size(axis)
        ends = count - 1
        head = lax.slice_in_dim(cells, 0, width, axis=dim)
        tail = lax.slice_in_dim(cells, cells.shape[dim] - width, cells.shape[dim], axis=dim)
        cells = jnp.concatenate(
            [
                lax.ppermute(tail, axis, [(i, (i + 1) % count) for i in range(ends)]),
                cells,
                lax.ppermute(head, axis, [((i + 1) % count, i) for i in range(ends)]),
            ],
            axis=dim,
        )
    return cells


def qk_norm(values, gain):
    rows = values.shape[0]
    shaped = values.astype(jnp.float32).reshape(rows, -1, HD)
    square = jnp.mean(shaped * shaped, axis=-1, keepdims=True)
    return (shaped * lax.rsqrt(square + EPS) * gain).reshape(rows, -1).astype(jnp.bfloat16)


def layout(image_tokens, text_tokens, positions):
    lengths = TXT + image_tokens
    ends = jnp.cumsum(lengths)
    starts = ends - lengths
    inside = (positions >= 0) & (positions < ends[-1])
    owner = jnp.sum((positions[:, None] >= ends[None, :]).astype(jnp.int32), axis=1)
    match = owner[:, None] == jnp.arange(lengths.shape[0], dtype=jnp.int32)[None, :]
    first = jnp.sum(jnp.where(match, starts[None, :], 0), axis=1)
    count = jnp.sum(jnp.where(match, text_tokens[None, :], 0), axis=1)
    offset = positions - first
    usable = inside & ((offset >= TXT) | (offset < count))
    owner = jnp.where(inside, owner, -1)
    return (owner, usable)


def attend(q_rows, k_rows, v_rows, q_owner, k_owner, k_usable):
    rows = q_rows.shape[0]
    heads = q_rows.shape[1] // HD
    q_heads = q_rows.reshape(rows, heads, HD)
    k_heads = k_rows.reshape(k_rows.shape[0], heads, HD)
    v_heads = v_rows.reshape(v_rows.shape[0], heads, HD)
    scores = jnp.einsum("qhd,khd->hqk", q_heads, k_heads, preferred_element_type=jnp.float32) * (
        1.0 / HD**0.5
    )
    allowed = (q_owner[:, None] == k_owner[None, :]) & k_usable[None, :]
    scores = jnp.where(allowed[None], scores, -1e30)
    top = jnp.max(scores, axis=-1, keepdims=True)
    weights = jnp.where(allowed[None], jnp.exp(scores - top), 0.0)
    total = jnp.sum(weights, axis=-1, keepdims=True)
    probs = (weights / total).astype(jnp.bfloat16)
    result = jnp.einsum("hqk,khd->qhd", probs, v_heads, preferred_element_type=jnp.float32)
    return result.reshape(rows, heads * HD).astype(jnp.bfloat16)


def local(q_in, k_in, v_in, q_gain, k_gain, image_tokens, text_tokens):
    q_norm = qk_norm(q_in, q_gain)
    k_norm = qk_norm(k_in, k_gain)
    q_heads, k_heads, v_heads = (
        lax.all_to_all(q_norm, "seq", split_axis=1, concat_axis=0, tiled=True),
        lax.all_to_all(k_norm, "seq", split_axis=1, concat_axis=0, tiled=True),
        lax.all_to_all(v_in, "seq", split_axis=1, concat_axis=0, tiled=True),
    )
    group = q_heads.shape[0]
    mean_image = group // 2 - TXT
    reach = TXT + mean_image + mean_image // 2 - 1
    block = min(512, group)
    paired = jnp.stack((k_heads, v_heads))
    extended = with_halo(paired, (("dp", 1),), reach)
    base = lax.axis_index("dp") * group
    q_owner, q_usable = layout(image_tokens, text_tokens, base + jnp.arange(group, dtype=jnp.int32))
    k_owner, k_usable = layout(
        image_tokens, text_tokens, base - reach + jnp.arange(group + 2 * reach, dtype=jnp.int32)
    )

    def one_block(index):
        start = index * block
        span = block + 2 * reach
        return attend(
            lax.dynamic_slice_in_dim(q_heads, start, block, 0),
            lax.dynamic_slice_in_dim(extended[0], start, span, 0),
            lax.dynamic_slice_in_dim(extended[1], start, span, 0),
            lax.dynamic_slice_in_dim(q_owner, start, block, 0),
            lax.dynamic_slice_in_dim(k_owner, start, span, 0),
            lax.dynamic_slice_in_dim(k_usable, start, span, 0),
        )

    blocks = lax.map(one_block, jnp.arange(group // block, dtype=jnp.int32))
    out_heads = blocks.reshape(group, q_heads.shape[1])
    return lax.all_to_all(out_heads, "seq", split_axis=0, concat_axis=1, tiled=True)


def solution(mesh):
    placed = (
        P(("dp", "seq"), None),
        P(("dp", "seq"), None),
        P(("dp", "seq"), None),
        P(),
        P(),
        P(),
        P(),
    )
    return jax.shard_map(
        local, mesh=mesh, in_specs=placed, out_specs=P(("dp", "seq"), None), check_vma=False
    )
```

profile of v0, /device:TPU:1, one launch (start us, length us, event | category | flops | bytes accessed | tf_op | source)
XLA Modules:
  0.0 180.2 jit_solution(11680995446446178259)
XLA Ops:
  0.0 1.3 fusion.11
  1.3 0.3 copy.121
  1.6 0.5 reduce_sum.63
  2.2 0.1 copy.97
  2.3 0.5 mul.74
  2.8 0.4 fusion.13
  3.2 1.2 copy.98
  4.4 6.8 %all-to-all-start = ((bf16[128,8,384]{0,2,1:T(8,128)(2,1)}), bf16[128,8,384]{0,2,1:T(8,128)(2,1)S(1)}, u32[]{:S(2)}, u32[]{:S(2)}) async-start(bf16[128,8,384]{0,2,1:T(8,128)(2,1)} %bitcast.7), calls=%async_computation | async-start | bytes 1572864 | tf_op jit(solution)/shard_map/all_to_all | solution.py:76
  11.2 1.1 copy.100
  12.3 0.2 fusion.14
  12.5 0.3 copy.123
  12.8 0.5 reduce_sum.68
  13.3 0.1 copy.108
  13.5 0.5 mul.84
  14.0 0.4 fusion.16
  14.4 9.1 %all-to-all-done = bf16[128,8,384]{0,2,1:T(8,128)(2,1)S(1)} async-done(((bf16[128,8,384]{0,2,1:T(8,128)(2,1)}), bf16[128,8,384]{0,2,1:T(8,128)(2,1)S(1)}, u32[]{:S(2)}, u32[]{:S(2)}) %all-to-all-start) | async-done | bytes 786464 | tf_op jit(solution)/shard_map/all_to_all | solution.py:76
  23.5 4.3 %all-to-all-start.1 = ((bf16[128,8,384]{0,2,1:T(8,128)(2,1)}), bf16[128,8,384]{0,2,1:T(8,128)(2,1)S(1)}, u32[]{:S(2)}, u32[]{:S(2)}) async-start(bf16[128,8,384]{0,2,1:T(8,128)(2,1)} %bitcast.10), calls=%async_computation.1 | async-start | bytes 1572864 | tf_op jit(solution)/shard_map/all_to_all | solution.py:77
  28.0 0.1 reduce
  28.1 1.2 copy.109
  29.3 0.2 convert_reduce_fusion
  29.5 0.4 copy.99
  29.9 10.3 %all-to-all-done.1 = bf16[128,8,384]{0,2,1:T(8,128)(2,1)S(1)} async-done(((bf16[128,8,384]{0,2,1:T(8,128)(2,1)}), bf16[128,8,384]{0,2,1:T(8,128)(2,1)S(1)}, u32[]{:S(2)}, u32[]{:S(2)}) %all-to-all-start.1) | async-done | bytes 786464 | tf_op jit(solution)/shard_map/all_to_all | solution.py:77
  40.1 4.3 %all-to-all-start.2 = ((bf16[128,8,384]{0,2,1:T(8,128)(2,1)}), bf16[128,8,384]{0,2,1:T(8,128)(2,1)S(1)}, u32[]{:S(2)}, u32[]{:S(2)}) async-start(bf16[128,8,384]{0,2,1:T(8,128)(2,1)} %bitcast.16), calls=%async_computation.2 | async-start | bytes 1572864 | tf_op jit(solution)/shard_map/all_to_all | solution.py:75
  44.4 0.4 copy.101
  44.8 0.5 fusion.18
  45.3 2.1 %copy.102 = bf16[2,703,384]{2,0,1:T(2,128)(2,1)} copy(bf16[2,703,384]{2,1,0:T(8,128)(2,1)S(1)} %get-tuple-element.113) | data formatting | bytes 2159616 | tf_op jit(solution)/shard_map/slice | solution.py:18
  47.5 3.8 %collective-permute-start = (bf16[2,703,384]{2,0,1:T(2,128)(2,1)}, bf16[2,703,384]{2,0,1:T(2,128)(2,1)}, u32[]{:S(2)}, u32[]{:S(2)}) collective-permute-start(bf16[2,703,384]{2,0,1:T(2,128)(2,1)} %copy.102), channel_id=1, source_target_pairs={{0,8},{8,16},{16,24},{24,32},{32,40},{40,48},{48,56},{56,64},{64,7... | collective-permute-start | bytes 3239432 | tf_op jit(solution)/shard_map/ppermute | solution.py:21
  51.2 2.1 %copy.103 = bf16[2,703,384]{2,0,1:T(2,128)(2,1)} copy(bf16[2,703,384]{2,1,0:T(8,128)(2,1)S(1)} %get-tuple-element.112) | data formatting | bytes 2159616 | tf_op jit(solution)/shard_map/slice | solution.py:17
  53.3 1.5 collective-permute-start.1
  54.8 0.3 select_reduce_fusion.1
  55.2 0.5 slice.24
  55.8 0.6 and_select_fusion
  56.4 0.6 broadcast_select_fusion
  57.0 0.6 or_and_fusion
  57.7 1.2 copy.110
  58.9 0.2 pad_maximum_fusion
  59.1 14.6 %collective-permute-done = bf16[2,703,384]{2,0,1:T(2,128)(2,1)} collective-permute-done((bf16[2,703,384]{2,0,1:T(2,128)(2,1)}, bf16[2,703,384]{2,0,1:T(2,128)(2,1)}, u32[]{:S(2)}, u32[]{:S(2)}) %collective-permute-start) | collective-permute-done | bytes 1079840 | tf_op jit(solution)/shard_map/ppermute | solution.py:21
  73.7 1.4 copy.104
  75.1 5.5 %collective-permute-done.1 = bf16[2,703,384]{2,0,1:T(2,128)(2,1)} collective-permute-done((bf16[2,703,384]{2,0,1:T(2,128)(2,1)}, bf16[2,703,384]{2,0,1:T(2,128)(2,1)}, u32[]{:S(2)}, u32[]{:S(2)}) %collective-permute-start.1) | collective-permute-done | bytes 1079840 | tf_op jit(solution)/shard_map/ppermute | solution.py:23
  80.6 2.4 %copy.105 = bf16[2,703,384]{2,1,0:T(8,128)(2,1)} copy(bf16[2,703,384]{2,0,1:T(2,128)(2,1)} %collective-permute-done.1) | data formatting | bytes 2159616 | tf_op jit(solution)/shard_map/ppermute | solution.py:23
  83.0 17.4 %concatenate.3 = bf16[2,2430,384]{2,1,0:T(8,128)(2,1)} concatenate(bf16[2,703,384]{2,1,0:T(8,128)(2,1)S(1)} %copy.104, bf16[2,1024,384]{2,1,0:T(8,128)(2,1)S(1)} %pad_maximum_fusion, bf16[2,703,384]{2,1,0:T(8,128)(2,1)} %copy.105), dimensions={1} | concatenate | bytes 7464960 | tf_op jit(solution)/shard_map/concatenate | solution.py:19
  100.4 6.0 %copy.111 = bf16[2,2430,384]{1,2,0:T(8,128)(2,1)} copy(bf16[2,2430,384]{2,1,0:T(8,128)(2,1)} %concatenate.3) | data formatting | bytes 7464960 | tf_op jit(solution)/shard_map/while | solution.py:103
  106.4 54.4 %while.10 = (s32[]{:T(128)}, bf16[2,512,384]{2,1,0:T(8,128)(2,1)}, bf16[2,2430,384]{1,2,0:T(8,128)(2,1)}, s32[2]{0:T(128)S(1)}, s32[1024]{0:T(1024)S(1)}, /*inde...) while((s32[]{:T(128)}, bf16[2,512,384]{2,1,0:T(8,128)(2,1)}, ...), condition=%wide.region_10.11_spmd, body=%wide.region_7.10_spmd.sunk | while | flops 1531161472 | bytes 55252380 | solution.py:103
  106.4 0.6 dynamic_slice.33
  107.8 1.7 compare_and_fusion.2
  109.4 2.3 %fusion.39 = (bf16[1,2430,384]{1,2,0:T(8,128)(2,1)S(1)}, bf16[1,2430,384]{1,2,0:T(8,128)(2,1)S(1)}) fusion(bf16[2,2430,384]{1,2,0:T(8,128)(2,1)} %get-tuple-element.203), kind=kLoop, calls=%fused_computation.55.clone.1 | loop fusion | bytes 7464960 | tf_op jit(solution)/shard_map/while/body/eval_jaxpr/slice | solution.py:96
  111.8 1.3 constant_dynamic-slice_fusion.5
  113.2 1.0 copy.129
  114.2 11.6 %fusion.40 = (f32[3,512]{1,0:T(4,128)S(1)}, f32[3,512,1918]{2,1,0:T(8,128)}) fusion(pred[512,1918]{1,0:T(8,128)(4,1)} %compare_and_fusion.2, bf16[512,3,128]{0,2,1:T(8,128)(2,1)} %bitcast.64, bf16[1918,3,128]{0,2,1:T(8,128)(2,1)S(1)} %bitcast.63), kind=kOutput, calls=%fused_computation.56.clone.1 | convolution fusion | flops 768920448 | bytes 14638592 | tf_op jit(solution)/shard_map/while/body/eval_jaxpr/sub | solution.py:64
  125.8 6.6 %fusion.41 = bf16[3,128,512]{2,1,0:T(8,128)(2,1)S(1)} fusion(bf16[1918,3,128]{0,2,1:T(8,128)(2,1)S(1)} %bitcast.62, f32[3,512,1918]{2,1,0:T(8,128)} %get-tuple-element.173, f32[3,512]{1,0:T(4,128)S(1)} %get-tuple-element.174), kind=kOutput, calls=%fused_computation.10.clone.1 | convolution fusion | flops 760276992 | bytes 13656576 | tf_op jit(solution)/shard_map/while/body/eval_jaxpr/hqk,khd->qhd/dot_general | solution.py:67
  132.4 0.2 copy.130
  132.7 0.9 copy-done.6
  133.6 0.6 dynamic_slice.33
  135.0 1.7 compare_and_fusion.2
  136.6 2.3 %fusion.39 = (bf16[1,2430,384]{1,2,0:T(8,128)(2,1)S(1)}, bf16[1,2430,384]{1,2,0:T(8,128)(2,1)S(1)}) fusion(bf16[2,2430,384]{1,2,0:T(8,128)(2,1)} %get-tuple-element.203), kind=kLoop, calls=%fused_computation.55.clone.1 | loop fusion | bytes 7464960 | tf_op jit(solution)/shard_map/while/body/eval_jaxpr/slice | solution.py:96
  139.0 1.3 constant_dynamic-slice_fusion.5
  140.4 1.0 copy.129
  141.3 11.6 %fusion.40 = (f32[3,512]{1,0:T(4,128)S(1)}, f32[3,512,1918]{2,1,0:T(8,128)}) fusion(pred[512,1918]{1,0:T(8,128)(4,1)} %compare_and_fusion.2, bf16[512,3,128]{0,2,1:T(8,128)(2,1)} %bitcast.64, bf16[1918,3,128]{0,2,1:T(8,128)(2,1)S(1)} %bitcast.63), kind=kOutput, calls=%fused_computation.56.clone.1 | convolution fusion | flops 768920448 | bytes 14638592 | tf_op jit(solution)/shard_map/while/body/eval_jaxpr/sub | solution.py:64
  153.0 6.6 %fusion.41 = bf16[3,128,512]{2,1,0:T(8,128)(2,1)S(1)} fusion(bf16[1918,3,128]{0,2,1:T(8,128)(2,1)S(1)} %bitcast.62, f32[3,512,1918]{2,1,0:T(8,128)} %get-tuple-element.173, f32[3,512]{1,0:T(4,128)S(1)} %get-tuple-element.174), kind=kOutput, calls=%fused_computation.10.clone.1 | convolution fusion | flops 760276992 | bytes 13656576 | tf_op jit(solution)/shard_map/while/body/eval_jaxpr/hqk,khd->qhd/dot_general | solution.py:67
  159.6 0.2 copy.130
  159.9 0.9 copy-done.6
  160.8 17.8 %all_to_all.70 = bf16[8,128,384]{2,1,0:T(8,128)(2,1)S(1)} all-to-all(bf16[8,128,384]{2,1,0:T(8,128)(2,1)} %bitcast.77), channel_id=1, replica_groups=mesh['dp'=32,'seq'=8] {'seq'}, dimensions={0} | all-to-all | bytes 1572864 | tf_op jit(solution)/shard_map/all_to_all | solution.py:105
  178.6 0.4 copy.114
  179.0 1.2 copy.115
  (50 shorter events, 1.2 us)
Async XLA Ops:
  0.0 2.3 %copy-start = (f32[128]{0:T(128)S(1)}, f32[128]{0:T(128)}, u32[]{:S(2)}) copy-start(f32[128]{0:T(128)} %param.13) | copy-start | bytes 1540
  1.6 1.2 copy-start.2
  3.2 8.0 %copy-start.4 = (bf16[128,3072]{1,0:T(8,128)(2,1)S(1)}, bf16[128,3072]{1,0:T(8,128)(2,1)}, u32[]{:S(2)}) copy-start(bf16[128,3072]{1,0:T(8,128)(2,1)} %param.11) | copy-start | bytes 2359300
  4.4 8.0 %copy-start.3 = (bf16[128,3072]{1,0:T(8,128)(2,1)S(1)}, bf16[128,3072]{1,0:T(8,128)(2,1)}, u32[]{:S(2)}) copy-start(bf16[128,3072]{1,0:T(8,128)(2,1)} %param.9) | copy-start | bytes 2359300
  4.4 19.1 %all-to-all-start = ((bf16[128,8,384]{0,2,1:T(8,128)(2,1)}), bf16[128,8,384]{0,2,1:T(8,128)(2,1)S(1)}, u32[]{:S(2)}, u32[]{:S(2)}) async-start(bf16[128,8,384]{0,2,1:T(8,128)(2,1)} %bitcast.7), calls=%async_computation | async-start | bytes 1572864 | tf_op jit(solution)/shard_map/all_to_all | solution.py:76
  12.8 0.7 copy-start.8
  14.4 13.4 %copy-start.9 = (s32[64]{0:T(128)S(1)}, s32[64]{0:T(128)}, u32[]{:S(2)}) copy-start(s32[64]{0:T(128)} %param.14) | copy-start | bytes 772
  23.5 16.6 %all-to-all-start.1 = ((bf16[128,8,384]{0,2,1:T(8,128)(2,1)}), bf16[128,8,384]{0,2,1:T(8,128)(2,1)S(1)}, u32[]{:S(2)}, u32[]{:S(2)}) async-start(bf16[128,8,384]{0,2,1:T(8,128)(2,1)} %bitcast.10), calls=%async_computation.1 | async-start | bytes 1572864 | tf_op jit(solution)/shard_map/all_to_all | solution.py:77
  40.1 17.6 %all-to-all-start.2 = ((bf16[128,8,384]{0,2,1:T(8,128)(2,1)}), bf16[128,8,384]{0,2,1:T(8,128)(2,1)S(1)}, u32[]{:S(2)}, u32[]{:S(2)}) async-start(bf16[128,8,384]{0,2,1:T(8,128)(2,1)} %bitcast.16), calls=%async_computation.2 | async-start | bytes 1572864 | tf_op jit(solution)/shard_map/all_to_all | solution.py:75
  47.5 7.4 %copy-start.7 = (s32[64]{0:T(128)S(1)}, s32[64]{0:T(128)}, u32[]{:S(2)}) copy-start(s32[64]{0:T(128)} %param.15) | copy-start | bytes 772
  47.5 26.3 %collective-permute-start = (bf16[2,703,384]{2,0,1:T(2,128)(2,1)}, bf16[2,703,384]{2,0,1:T(2,128)(2,1)}, u32[]{:S(2)}, u32[]{:S(2)}) collective-permute-start(bf16[2,703,384]{2,0,1:T(2,128)(2,1)} %copy.102), channel_id=1, source_target_pairs={{0,8},{8,16},{16,24},{24,32},{32,40},{40,48},{48,56},{56,64},{64,7... | collective-permute-start | bytes 3239432 | tf_op jit(solution)/shard_map/ppermute | solution.py:21
  53.3 27.3 %collective-permute-start.1 = (bf16[2,703,384]{2,0,1:T(2,128)(2,1)}, bf16[2,703,384]{2,0,1:T(2,128)(2,1)}, u32[]{:S(2)}, u32[]{:S(2)}) collective-permute-start(bf16[2,703,384]{2,0,1:T(2,128)(2,1)} %copy.103), channel_id=1, source_target_pairs={{8,0},{16,8},{24,16},{32,24},{40,32},{48,40},{56,48},{64,56},{72,6... | collective-permute-start | bytes 3239432 | tf_op jit(solution)/shard_map/ppermute | solution.py:23
  111.8 1.3 copy-start.1
  125.8 6.8 %copy-start.5 = (bf16[2,512,384]{2,1,0:T(8,128)(2,1)S(1)}, bf16[2,512,384]{2,1,0:T(8,128)(2,1)}, u32[]{:S(2)}) copy-start(bf16[2,512,384]{2,1,0:T(8,128)(2,1)} %get-tuple-element.189) | copy-start | bytes 2359300 | tf_op jit(solution)/shard_map/while
  132.7 0.9 copy-start.6
  139.0 1.3 copy-start.1
  153.0 6.8 %copy-start.5 = (bf16[2,512,384]{2,1,0:T(8,128)(2,1)S(1)}, bf16[2,512,384]{2,1,0:T(8,128)(2,1)}, u32[]{:S(2)}) copy-start(bf16[2,512,384]{2,1,0:T(8,128)(2,1)} %get-tuple-element.189) | copy-start | bytes 2359300 | tf_op jit(solution)/shard_map/while
  159.9 0.9 copy-start.6
where the time goes:
time: 183 us; the launch traced here: 180 us
  local copies, waits for them, and re-layouts  54.2 us (30%)
  waiting for transfers between devices  39.5 us (22%)
  matrix products  36.4 us (20%)
  starting transfers between devices  20.7 us (11%)
  blocking collectives  17.8 us (10%)
  other arithmetic  9.94 us (5%)
    sub x2, matrix products, attend(): weights = jnp.where(allowed[None], jnp.exp(scores - top), 0.0)  23.3 us
    all_to_all x1, blocking collectives, local(): lax.all_to_all(out_heads, 'seq', split_axis=0, concat_axis=1, tiled=True)  17.8 us
    concatenate x1, local copies, waits for them, and re-layouts, with_halo(): jnp.concatenate([lax.ppermute(tail, axis, [(i, (i + 1) % count) for i in...  17.4 us
    ppermute x1, waiting for transfers between devices, with_halo(): lax.ppermute(tail, axis, [(i, (i + 1) % count) for i in range(ends)])  14.6 us
    dot_general x2, matrix products, attend(): jnp.einsum('hqk,khd->qhd', probs, v_heads, preferred_element_type=jnp.flo...  13.2 us
    all_to_all x1, waiting for transfers between devices, local(): lax.all_to_all(v_in, 'seq', split_axis=1, concat_axis=0, tiled=True)  10.3 us
    all_to_all x1, waiting for transfers between devices, local(): lax.all_to_all(k_norm, 'seq', split_axis=1, concat_axis=0, tiled=True)  9.11 us
    all_to_all x1, starting transfers between devices, local(): lax.all_to_all(k_norm, 'seq', split_axis=1, concat_axis=0, tiled=True)  6.82 us
  transfers between devices with their start and end apart: 5, of which 4 were waited for; matrix products, arithmetic and copies ran while one was open for 9% of the time, Pallas kernels for 0%

commit v1 on v0

v1 whole, which is shorter than its diff:
```python
import functools

import jax
import jax.numpy as jnp
from jax import lax
from jax.experimental import pallas as pl
from jax.experimental.pallas import tpu as pltpu
from jax.sharding import PartitionSpec as P

MESH = pl.DeviceIdType.MESH
BF16 = jnp.bfloat16
F32 = jnp.float32

HD = 128
TXT = 128
EPS = 1e-06
SEQ = 8
SLOTS = 3
ROWS = 128
GROUP = SEQ * ROWS
HALO = 704
EXT = GROUP + 2 * HALO
BLOCK = 256
WINDOW = BLOCK + 2 * HALO
SAMPLES = 64

MARK_Q = 64.0
MARK_K = 128.0
SCALE = 1.4426950408889634 / HD**0.5

OTHERS = ((1, 0), (1, 1), (-1, 0), (-1, 1), (2, 0), (2, 1), (0, 1))
ARRIVAL = ((0, 0), (0, 1), (1, 0), (-1, 0), (1, 1), (-1, 1), (2, 0), (2, 1))
NT = (((1,), (1,)), ((), ()))


def partner(s, dx, dc):
    return lax.rem(s // 2 + dx + 4, 4) * 2 + lax.rem(s % 2 + dc, 2)


def kernel(
    groups,
    q_in, k_in, v_in, q_gain, k_gain, image, text,
    out,
    q_buf, k_buf, v_buf, kv_src, q_src, kv, q_all, o_buf, mark_q, mark_k, ints,
    load_sem, own_sem, kv_send, kv_recv, q_send, q_recv,
    left_send, left_recv, right_send, right_recv, out_send, out_recv, out_own,
):
    dp = lax.axis_index("dp")
    s = lax.axis_index("seq")
    after = lax.rem(dp + 1, groups)
    before = lax.rem(dp + groups - 1, groups)

    barrier = pltpu.get_barrier_semaphore()
    for dx, dc in OTHERS:
        pl.semaphore_signal(barrier, 1, device_id=(dp, partner(s, dx, dc)), device_id_type=MESH)
    pl.semaphore_signal(barrier, 1, device_id=(after, s), device_id_type=MESH)
    pl.semaphore_signal(barrier, 1, device_id=(before, s), device_id_type=MESH)

    loads = [
        pltpu.make_async_copy(src, dst, load_sem.at[i])
        for i, (src, dst) in enumerate(((k_in, k_buf), (v_in, v_buf), (q_in, q_buf)))
    ]
    for load in loads:
        load.start()

    def cols(head):
        return pl.ds(pl.multiple_of(head * HD, HD), HD)

    def normed(buf, head, gain):
        x = buf[:, cols(head)].astype(F32)
        square = jnp.sum(x * x, axis=1, keepdims=True) * (1.0 / HD)
        return (x * lax.rsqrt(square + EPS) * gain[...]).astype(BF16)

    def remote(src, dst, send, recv, dev):
        return pltpu.make_async_remote_copy(
            src_ref=src, dst_ref=dst, send_sem=send, recv_sem=recv, device_id=dev, device_id_type=MESH
        )

    def kv_rows(j, first, count):
        return kv.at[j, :, pl.ds(pl.multiple_of(first, 64), count), :]

    def kv_copy(j, to, source, index):
        return remote(
            kv_src.at[to * SLOTS + j], kv_rows(j, HALO + source * ROWS, ROWS),
            kv_send.at[j, index], kv_recv.at[j, source], (dp, to),
        )

    def q_copy(j, to, source, index):
        return remote(
            q_src.at[to * SLOTS + j], q_all.at[j, pl.ds(pl.multiple_of(source * ROWS, ROWS), ROWS), :],
            q_send.at[j, index], q_recv.at[j, source], (dp, to),
        )

    def left_copy(j, source, skip):
        first = source * ROWS + skip
        return remote(
            kv_rows(j, HALO + first, ROWS - skip), kv_rows(j, first - (GROUP - HALO), ROWS - skip),
            left_send.at[j, source], left_recv.at[j, source], (after, s),
        )

    def right_copy(j, source, count):
        first = source * ROWS
        return remote(
            kv_rows(j, HALO + first, count), kv_rows(j, HALO + GROUP + first, count),
            right_send.at[j, source], right_recv.at[j, source], (before, s),
        )

    def out_copy(j, to, source):
        return remote(
            o_buf.at[j, pl.ds(pl.multiple_of(to * ROWS, ROWS), ROWS), :], out.at[:, cols(source * SLOTS + j)],
            out_send.at[j, to], out_recv.at[j, source], (dp, to),
        )

    def own_kv(j):
        return pltpu.make_async_copy(kv_src.at[s * SLOTS + j], kv_rows(j, HALO + s * ROWS, ROWS), own_sem.at[0, j])

    def own_q(j):
        return pltpu.make_async_copy(
            q_src.at[s * SLOTS + j], q_all.at[j, pl.ds(pl.multiple_of(s * ROWS, ROWS), ROWS), :], own_sem.at[1, j]
        )

    def own_out(j):
        return pltpu.make_async_copy(
            o_buf.at[j, pl.ds(pl.multiple_of(s * ROWS, ROWS), ROWS), :], out.at[:, cols(s * SLOTS + j)], out_own.at[j]
        )

    def send_kv(j):
        for index, (dx, dc) in enumerate(OTHERS):
            kv_copy(j, partner(s, dx, dc), s, index).start()

    def send_q(j):
        for index, (dx, dc) in enumerate(OTHERS):
            q_copy(j, partner(s, dx, dc), s, index).start()

    def pass_on(j):
        for dx, dc in ARRIVAL:
            source = partner(s, dx, dc)
            if (dx, dc) == (0, 0):
                own_kv(j).wait()
            else:
                kv_copy(j, s, source, 0).wait_recv()

            @pl.when(source >= 3)
            def _():
                left_copy(j, source, 0).start()

            @pl.when(source == 2)
            def _():
                left_copy(j, source, 64).start()

            @pl.when(source <= 4)
            def _():
                right_copy(j, source, ROWS).start()

            @pl.when(source == 5)
            def _():
                right_copy(j, source, 64).start()

    def attend(j):
        for dx, dc in OTHERS:
            q_copy(j, s, partner(s, dx, dc), 0).wait_recv()
        own_q(j).wait()
        for source in range(2, SEQ):
            left_copy(j, source, 64 if source == 2 else 0).wait_recv()
        for source in range(6):
            right_copy(j, source, 64 if source == 5 else ROWS).wait_recv()
        for i in range(GROUP // BLOCK):
            rows, window = pl.ds(i * BLOCK, BLOCK), pl.ds(i * BLOCK, WINDOW)
            q = jnp.concatenate([q_all[j, rows, :], mark_q[rows, :]], axis=1)
            k = jnp.concatenate([kv[j, 0, window, :], mark_k[window, :]], axis=1)
            v = kv[j, 1, window, :]
            scores = lax.dot_general(q, k, NT, preferred_element_type=F32)
            top = jnp.max(scores, axis=1, keepdims=True)
            weights = jnp.exp2((scores - top) * SCALE).astype(BF16)
            sums = jnp.dot(weights, jnp.concatenate([v, jnp.ones_like(v)], axis=1), preferred_element_type=F32)
            o_buf[j, rows, :] = (sums[:, :HD] / sums[:, HD:]).astype(BF16)
        for dx, dc in OTHERS:
            out_copy(j, partner(s, dx, dc), s).start()
        own_out(j).start()

    loads[0].wait()
    loads[1].wait()

    def prepare_k(i, carry):
        for u in range(SLOTS):
            head = i * SLOTS + u
            kv_src[head, 0] = normed(k_buf, head, k_gain)
            kv_src[head, 1] = v_buf[:, cols(head)]
        return carry

    lax.fori_loop(0, SEQ, prepare_k, 0)
    pl.semaphore_wait(barrier, len(OTHERS) + 2)

    send_kv(0)
    for j in range(SLOTS):
        own_kv(j).start()
    loads[2].wait()

    def prepare_q(i, carry):
        for u in range(SLOTS):
            head = i * SLOTS + u
            q_src[head] = normed(q_buf, head, q_gain)
        return carry

    lax.fori_loop(0, SEQ, prepare_q, 0)
    send_q(0)
    send_kv(1)
    send_kv(2)
    send_q(1)
    send_q(2)
    for j in range(SLOTS):
        own_q(j).start()

    lane = lax.broadcasted_iota(jnp.int32, (8, HD), 1)
    ints[...] = jnp.zeros_like(ints)
    ints[0, :, :SAMPLES] = jnp.broadcast_to(image[...], (8, SAMPLES)) + TXT
    ints[1, :, :SAMPLES] = jnp.broadcast_to(text[...], (8, SAMPLES))
    lengths = ints[0]
    ends = lengths
    step = 1
    while step < SAMPLES:
        ends = ends + jnp.where(lane >= step, pltpu.roll(ends, step, 1), 0)
        step *= 2
    starts = (ends - lengths)[:1]
    ends = ends[:1]
    text_ends = starts + ints[1][:1]
    tokens = groups * GROUP

    def mark(i, carry):
        first = pl.multiple_of(i * 64, 64)
        position = dp * GROUP - HALO + first + lax.broadcasted_iota(jnp.int32, (64, HD), 0)
        position = jnp.where(position < 0, position + tokens, position)
        position = jnp.where(position >= tokens, position - tokens, position)
        inside = (position >= starts) & (position < ends)
        usable = inside & ((position >= starts + TXT) | (position < text_ends))
        mark_k[pl.ds(first, 64), :] = jnp.where(usable, MARK_K, 0.0).astype(BF16)

        @pl.when((i >= HALO // 64) & (i < (HALO + GROUP) // 64))
        def _():
            mark_q[pl.ds(pl.multiple_of(first - HALO, 64), 64), :] = jnp.where(inside, MARK_Q, 0.0).astype(BF16)

        return carry

    lax.fori_loop(0, EXT // 64, mark, 0)

    pass_on(0)
    pass_on(1)
    attend(0)
    pass_on(2)
    attend(1)
    attend(2)

    for j in range(SLOTS):
        for dx, dc in OTHERS:
            out_copy(j, s, partner(s, dx, dc)).wait_recv()
        own_out(j).wait()
    for j in range(SLOTS):
        for index, (dx, dc) in enumerate(OTHERS):
            kv_copy(j, partner(s, dx, dc), s, index).wait_send()
            q_copy(j, partner(s, dx, dc), s, index).wait_send()
            out_copy(j, partner(s, dx, dc), s).wait_send()
        for source in range(2, SEQ):
            left_copy(j, source, 64 if source == 2 else 0).wait_send()
        for source in range(6):
            right_copy(j, source, 64 if source == 5 else ROWS).wait_send()


def solution(mesh):
    groups = mesh.shape["dp"]
    dma = pltpu.SemaphoreType.DMA

    def local(q_in, k_in, v_in, q_gain, k_gain, image_tokens, text_tokens):
        rows, width = q_in.shape
        heads = width // HD
        any_space = pl.BlockSpec(memory_space=pl.ANY)
        vmem = pl.BlockSpec(memory_space=pltpu.VMEM)
        return pl.pallas_call(
            functools.partial(kernel, groups),
            out_shape=jax.ShapeDtypeStruct((rows, width), BF16),
            in_specs=[any_space] * 3 + [vmem] * 4,
            out_specs=any_space,
            scratch_shapes=[
                pltpu.VMEM((rows, width), BF16),
                pltpu.VMEM((rows, width), BF16),
                pltpu.VMEM((rows, width), BF16),
                pltpu.VMEM((heads, 2, rows, HD), BF16),
                pltpu.VMEM((heads, rows, HD), BF16),
                pltpu.VMEM((SLOTS, 2, EXT, HD), BF16),
                pltpu.VMEM((SLOTS, GROUP, HD), BF16),
                pltpu.VMEM((SLOTS, GROUP, HD), BF16),
                pltpu.VMEM((GROUP, HD), BF16),
                pltpu.VMEM((EXT, HD), BF16),
                pltpu.VMEM((2, 8, HD), jnp.int32),
                dma((3,)),
                dma((2, SLOTS)),
                dma((SLOTS, SEQ)),
                dma((SLOTS, SEQ)),
                dma((SLOTS, SEQ)),
                dma((SLOTS, SEQ)),
                dma((SLOTS, SEQ)),
                dma((SLOTS, SEQ)),
                dma((SLOTS, SEQ)),
                dma((SLOTS, SEQ)),
                dma((SLOTS, SEQ)),
                dma((SLOTS, SEQ)),
                dma((SLOTS,)),
            ],
            compiler_params=pltpu.CompilerParams(
                collective_id=0, has_side_effects=True, vmem_limit_bytes=48 * 1024 * 1024
            ),
            cost_estimate=pl.CostEstimate(flops=4_000_000_000, bytes_accessed=4_000_000, transcendentals=5_000_000),
            name="joint_attention",
        )(
            q_in, k_in, v_in,
            q_gain.reshape(1, HD), k_gain.reshape(1, HD),
            image_tokens.reshape(1, SAMPLES), text_tokens.reshape(1, SAMPLES),
        )

    split = P(("dp", "seq"), None)
    return jax.shard_map(
        local,
        mesh=mesh,
        in_specs=(split, split, split, P(), P(), P(), P()),
        out_specs=split,
        check_vma=False,
    )
```

time: 183 us -> 56.7 us (0.31); the launches traced: 180 us -> 56.5 us
  Pallas kernels: 0 us -> 51.5 us
  local copies, waits for them, and re-layouts: 54.2 us -> 4.97 us
  waiting for transfers between devices: 39.5 us -> 0 us
  matrix products: 36.4 us -> 0 us
  starting transfers between devices: 20.7 us -> 0 us
  blocking collectives: 17.8 us -> 0 us
  other arithmetic: 9.94 us -> 0 us
    pallas_call x0 -> x1, Pallas kernels: none -> 51.5 us  [local(): pl.pallas_call(functools.partial(kernel, groups), out_shape=jax.ShapeDtyp...]
    sub x2 -> x0, matrix products: 23.3 us -> none  [attend(): weights = jnp.where(allowed[None], jnp.exp(scores - top), 0.0)]
    ppermute x2 -> x0, waiting for transfers between devices: 20.1 us -> none  [the longest x1 14.6 us: with_halo(): lax.ppermute(tail, axis, [(i, (i + 1) % count) for i in range(ends)])]
    all_to_all x3 -> x0, waiting for transfers between devices: 19.4 us -> none  [the longest x1 10.3 us: local(): lax.all_to_all(v_in, 'seq', split_axis=1, concat_axis=0, tiled=True)]
    all_to_all x1 -> x0, blocking collectives: 17.8 us -> none  [local(): lax.all_to_all(out_heads, 'seq', split_axis=0, concat_axis=1, tiled=True)]
    concatenate x1 -> x0, local copies, waits for them, and re-layouts: 17.4 us -> none  [with_halo(): jnp.concatenate([lax.ppermute(tail, axis, [(i, (i + 1) % count) for i in...]
    all_to_all x3 -> x0, starting transfers between devices: 15.5 us -> none  [the longest x1 6.82 us: local(): lax.all_to_all(k_norm, 'seq', split_axis=1, concat_axis=0, tiled=True)]
    dot_general x2 -> x0, matrix products: 13.2 us -> none  [attend(): jnp.einsum('hqk,khd->qhd', probs, v_heads, preferred_element_type=jnp.flo...]
  transfers between devices with their start and end apart: 5 -> 0, of which waited for: 4 -> 0; matrix products, arithmetic and copies ran while one was open for 9% -> 0% of each run, Pallas kernels for 0% -> 0%
where the time goes in v1:
time: 56.7 us; the launch traced here: 56.5 us
  Pallas kernels  51.5 us (91%)
  local copies, waits for them, and re-layouts  4.97 us (9%)
    pallas_call x1, Pallas kernels, local(): pl.pallas_call(functools.partial(kernel, groups), out_shape=jax.ShapeDtyp...  51.5 us
    unnamed x15, local copies, waits for them, and re-layouts  4.97 us

profile of v1, /device:TPU:1, one launch (start us, length us, event | category | flops | bytes accessed | tf_op | source)
XLA Modules:
  0.0 56.5 jit_solution(5120354907928969419)
XLA Ops:
  0.0 0.0 copy-start.6
  0.0 0.0 copy-start.3
  0.0 0.0 copy-start.4
  0.0 0.0 copy-start.5
  0.0 0.6 %copy-done.6 = s32[64]{0:T(128)S(1)} copy-done((s32[64]{0:T(128)S(1)}, s32[64]{0:T(128)}, u32[]{:S(2)}) %copy-start.6) | copy-done | bytes 280
  0.7 0.0 copy-done.3
  0.7 0.0 copy-done.4
  0.7 0.0 copy-done.5
  0.7 0.0 copy-start
  0.7 1.1 %copy-done = bf16[128,3072]{1,0:T(8,128)(2,1)S(1)} copy-done((bf16[128,3072]{1,0:T(8,128)(2,1)S(1)}, bf16[128,3072]{1,0:T(8,128)(2,1)}, u32[]{:S(2)}) %copy-start) | copy-done | bytes 786456
  1.8 0.0 copy-start.1
  1.8 1.1 %copy-done.1 = bf16[128,3072]{1,0:T(8,128)(2,1)S(1)} copy-done((bf16[128,3072]{1,0:T(8,128)(2,1)S(1)}, bf16[128,3072]{1,0:T(8,128)(2,1)}, u32[]{:S(2)}) %copy-start.1) | copy-done | bytes 786456
  3.0 0.0 copy-start.2
  3.0 1.1 %copy-done.2 = bf16[128,3072]{1,0:T(8,128)(2,1)S(1)} copy-done((bf16[128,3072]{1,0:T(8,128)(2,1)S(1)}, bf16[128,3072]{1,0:T(8,128)(2,1)}, u32[]{:S(2)}) %copy-start.2) | copy-done | bytes 786456
  4.1 51.5 %joint_attention.1 = bf16[128,3072]{1,0:T(8,128)(2,1)S(1)} custom-call(bf16[128,3072]{1,0:T(8,128)(2,1)S(1)} %copy-done, bf16[128,3072]{1,0:T(8,128)(2,1)S(1)} %copy-done.1, bf16[128,3072]{1,0:T(8,128)(2,1)S(1)} %copy-done.2, f32[1,128]{1,0:T(1,128)S(1)} %bitcast.4, f32[1,128]{1,0:T(1,128)S(1)} %bitcast.5, s32[1,64]{1,0:T(1,128)S(1)} %bitcast.6, ...), custom_call_target="tpu_custom_call" | custom-call | flops 4000000000 | bytes 4000000 | tf_op jit(solution)/shard_map/joint_attention/pallas_call | solution.py:277
  55.6 0.9 %copy.9 = bf16[128,3072]{1,0:T(8,128)(2,1)} copy(bf16[128,3072]{1,0:T(8,128)(2,1)S(1)} %joint_attention.1) | data formatting | bytes 1572864
Async XLA Ops:
  0.0 0.7 %copy-start.6 = (s32[64]{0:T(128)S(1)}, s32[64]{0:T(128)}, u32[]{:S(2)}) copy-start(s32[64]{0:T(128)} %param.13) | copy-start | bytes 772
  0.0 0.7 %copy-start.3 = (f32[128]{0:T(128)S(1)}, f32[128]{0:T(128)}, u32[]{:S(2)}) copy-start(f32[128]{0:T(128)} %param.10) | copy-start | bytes 1540
  0.0 0.7 %copy-start.4 = (f32[128]{0:T(128)S(1)}, f32[128]{0:T(128)}, u32[]{:S(2)}) copy-start(f32[128]{0:T(128)} %param.11) | copy-start | bytes 1540
  0.0 0.7 %copy-start.5 = (s32[64]{0:T(128)S(1)}, s32[64]{0:T(128)}, u32[]{:S(2)}) copy-start(s32[64]{0:T(128)} %param.12) | copy-start | bytes 772
  0.7 1.1 %copy-start = (bf16[128,3072]{1,0:T(8,128)(2,1)S(1)}, bf16[128,3072]{1,0:T(8,128)(2,1)}, u32[]{:S(2)}) copy-start(bf16[128,3072]{1,0:T(8,128)(2,1)} %q_in.1) | copy-start | bytes 2359300
  1.8 1.1 %copy-start.1 = (bf16[128,3072]{1,0:T(8,128)(2,1)S(1)}, bf16[128,3072]{1,0:T(8,128)(2,1)}, u32[]{:S(2)}) copy-start(bf16[128,3072]{1,0:T(8,128)(2,1)} %k_in.1) | copy-start | bytes 2359300
  3.0 1.1 %copy-start.2 = (bf16[128,3072]{1,0:T(8,128)(2,1)S(1)}, bf16[128,3072]{1,0:T(8,128)(2,1)}, u32[]{:S(2)}) copy-start(bf16[128,3072]{1,0:T(8,128)(2,1)} %v_in.1) | copy-start | bytes 2359300

commit v2 on v1

v2 whole, which is shorter than its diff:
```python
import functools

import jax
import jax.numpy as jnp
from jax import lax
from jax.experimental import pallas as pl
from jax.experimental.pallas import tpu as pltpu
from jax.sharding import PartitionSpec as P

MESH = pl.DeviceIdType.MESH
BF16 = jnp.bfloat16
F32 = jnp.float32

HD = 128
TXT = 128
EPS = 1e-06
SEQ = 8
SLOTS = 3
ROWS = 128
GROUP = SEQ * ROWS
HALO = 704
EXT = GROUP + 2 * HALO
BLOCK = 256
WINDOW = BLOCK + 2 * HALO
SAMPLES = 64
VMEM_BYTES = 53 * 1024 * 1024
NORM_HEADS = 12
K, V = 0, 1

MARK_Q = 64.0
MARK_K = 128.0
SCALE = 1.4426950408889634 / HD**0.5

OTHERS = ((1, 0), (1, 1), (-1, 0), (-1, 1), (2, 0), (2, 1), (0, 1))
ARRIVAL = ((0, 0), (0, 1), (1, 0), (-1, 0), (1, 1), (-1, 1), (2, 0), (2, 1))
NT = (((1,), (1,)), ((), ()))


def partner(s, dx, dc):
    return lax.rem(s // 2 + dx + 4, 4) * 2 + lax.rem(s % 2 + dc, 2)


def kernel(
    groups,
    q_in, k_in, v_in, q_gain, k_gain, image, text,
    out,
    q_buf, k_buf, q_src, k_src, kv_all, q_all, o_buf, mark_q, mark_k, gains, image_buf, text_buf, ints,
    load_sem, own_sem, ready, x_send, z_send, v_recv, kv_recv, q_recv, halo_left, halo_right, out_recv,
):
    dp = lax.axis_index("dp")
    s = lax.axis_index("seq")
    has_after = dp < groups - 1
    has_before = dp > 0
    odd = lax.rem(dp, 2) == 1
    even = jnp.logical_not(odd)
    after = lax.rem(dp + 1, groups)
    before = lax.rem(dp + groups - 1, groups)

    barrier = pltpu.get_barrier_semaphore()
    for dx, dc in OTHERS:
        pl.semaphore_signal(barrier, 1, device_id=(dp, partner(s, dx, dc)), device_id_type=MESH)

    @pl.when(even & has_after)
    def _():
        pl.semaphore_signal(barrier, 1, device_id=(after, s), device_id_type=MESH)

    @pl.when(even & has_before)
    def _():
        pl.semaphore_signal(barrier, 1, device_id=(before, s), device_id_type=MESH)

    small = [
        pltpu.make_async_copy(src, dst, load_sem.at[i])
        for i, (src, dst) in enumerate(
            ((k_gain, gains.at[0]), (q_gain, gains.at[1]), (image, image_buf), (text, text_buf))
        )
    ]
    load_k = pltpu.make_async_copy(k_in, k_buf, load_sem.at[4])
    load_q = pltpu.make_async_copy(q_in, q_buf, load_sem.at[5])
    load_k.start()
    for copy in small:
        copy.start()
    load_q.start()

    def cols(head, count=1):
        return pl.ds(pl.multiple_of(head * HD, HD), count * HD)

    def block(first, count=ROWS):
        return pl.ds(pl.multiple_of(first, 64), count)

    def remote(src, dst, send, recv, dev):
        return pltpu.make_async_remote_copy(
            src_ref=src, dst_ref=dst, send_sem=send, recv_sem=recv, device_id=dev, device_id_type=MESH
        )

    def wait_all(ref, sem):
        pltpu.make_async_copy(ref, ref, sem).wait()

    def source_of(a):
        return k_src if a == K else v_in

    def kv_copy(a, j, to, source):
        recv = v_recv.at[source] if (a, j) == (V, 0) else kv_recv.at[a, j]
        return remote(
            source_of(a).at[:, cols(to * SLOTS + j)], kv_all.at[a, j, block(HALO + source * ROWS), :],
            x_send.at[a], recv, (dp, to),
        )

    def q_copy(j, to, source):
        return remote(
            q_src.at[:, cols(to * SLOTS + j)], q_all.at[j, block(source * ROWS), :],
            x_send.at[2], q_recv.at[j], (dp, to),
        )

    def out_copy(j, to, source):
        return remote(
            o_buf.at[j, block(to * ROWS), :], out.at[:, cols(source * SLOTS + j)],
            x_send.at[3], out_recv.at[j], (dp, to),
        )

    def pass_on(a, j, source, own=False):
        def rows(first, count):
            if own:
                return source_of(a).at[pl.ds(first, count), cols(s * SLOTS + j)]
            return kv_all.at[a, j, block(HALO + source * ROWS + first, count), :]

        def to_after(first, count):
            remote(
                rows(first, count), kv_all.at[a, j, block(source * ROWS + first - (GROUP - HALO), count), :],
                z_send.at[0], halo_left.at[j], (after, s),
            ).start()

        def to_before(count):
            remote(
                rows(0, count), kv_all.at[a, j, block(HALO + GROUP + source * ROWS, count), :],
                z_send.at[1], halo_right.at[j], (before, s),
            ).start()

        @pl.when((source >= 3) & has_after)
        def _():
            to_after(0, ROWS)

        @pl.when((source == 2) & has_after)
        def _():
            to_after(64, ROWS - 64)

        @pl.when((source <= 4) & has_before)
        def _():
            to_before(ROWS)

        @pl.when((source == 5) & has_before)
        def _():
            to_before(64)

    def pass_own():
        for j in range(SLOTS):
            for a in (V, K):
                pass_on(a, j, s, own=True)

    def own_kv(a, j):
        return pltpu.make_async_copy(
            source_of(a).at[:, cols(s * SLOTS + j)], kv_all.at[a, j, block(HALO + s * ROWS), :], own_sem.at[a]
        )

    def own_q(j):
        return pltpu.make_async_copy(
            q_src.at[:, cols(s * SLOTS + j)], q_all.at[j, block(s * ROWS), :], own_sem.at[2]
        )

    def own_out(j):
        return pltpu.make_async_copy(
            o_buf.at[j, block(s * ROWS), :], out.at[:, cols(s * SLOTS + j)], own_sem.at[3]
        )

    def normalize(buf, gain, to):
        def some(i, carry):
            for u in range(NORM_HEADS):
                where = cols(i * NORM_HEADS + u)
                x = buf[:, where].astype(F32)
                square = jnp.sum(x * x, axis=1, keepdims=True) * (1.0 / HD)
                to[:, where] = (x * lax.rsqrt(square + EPS) * gain).astype(BF16)
            return carry

        lax.fori_loop(0, SEQ * SLOTS // NORM_HEADS, some, 0)

    def attend(j):
        wait_all(q_all.at[0, pl.ds(0, len(OTHERS) * ROWS), :], q_recv.at[j])

        @pl.when(has_before)
        def _():
            wait_all(kv_all.at[K, 0, pl.ds(0, 2 * HALO), :], halo_left.at[j])

        @pl.when(has_after)
        def _():
            wait_all(kv_all.at[K, 0, pl.ds(0, 2 * HALO), :], halo_right.at[j])

        for i in range(GROUP // BLOCK):
            rows, window = pl.ds(i * BLOCK, BLOCK), pl.ds(i * BLOCK, WINDOW)
            q = jnp.concatenate([q_all[j, rows, :], mark_q[rows, :]], axis=1)
            k = jnp.concatenate([kv_all[K, j, window, :], mark_k[window, :]], axis=1)
            v = kv_all[V, j, window, :]
            scores = lax.dot_general(q, k, NT, preferred_element_type=F32)
            top = jnp.max(scores, axis=1, keepdims=True)
            weights = jnp.exp2((scores - top) * SCALE).astype(BF16)
            sums = jnp.dot(weights, jnp.concatenate([v, jnp.ones_like(v)], axis=1), preferred_element_type=F32)
            o_buf[j, rows, :] = (sums[:, :HD] / sums[:, HD:]).astype(BF16)
        for dx, dc in OTHERS:
            out_copy(j, partner(s, dx, dc), s).start()
        own_out(j).start()

    load_k.wait()
    for copy in small:
        copy.wait()
    normalize(k_buf, gains[0], k_src)

    @pl.when(even)
    def _():
        pl.semaphore_wait(barrier, len(OTHERS))

    @pl.when(odd & has_after)
    def _():
        pl.semaphore_wait(barrier, len(OTHERS) + 2)

    @pl.when(odd & jnp.logical_not(has_after))
    def _():
        pl.semaphore_wait(barrier, len(OTHERS) + 1)

    def send_kv(a, j):
        for dx, dc in OTHERS:
            kv_copy(a, j, partner(s, dx, dc), s).start()

    send_kv(V, 0)

    @pl.when(odd)
    def _():
        pl.semaphore_signal(ready, 1, device_id=(before, s), device_id_type=MESH)

    @pl.when(odd & has_after)
    def _():
        pl.semaphore_signal(ready, 1, device_id=(after, s), device_id_type=MESH)

    send_kv(K, 0)

    @pl.when(odd)
    def _():
        pass_own()

    for j in range(1, SLOTS):
        send_kv(V, j)
        send_kv(K, j)
    for j in range(SLOTS):
        own_kv(K, j).start()
        own_kv(V, j).start()
    load_q.wait()
    normalize(q_buf, gains[1], q_src)
    for j in range(SLOTS):
        for dx, dc in OTHERS:
            q_copy(j, partner(s, dx, dc), s).start()
        own_q(j).start()

    @pl.when(even & has_after & has_before)
    def _():
        pl.semaphore_wait(ready, 2)

    @pl.when(even & jnp.logical_not(has_after & has_before))
    def _():
        pl.semaphore_wait(ready, 1)

    @pl.when(even)
    def _():
        pass_own()

    for j in range(SLOTS):
        for a in (V, K):
            if (a, j) != (V, 0):
                wait_all(kv_all.at[a, 0, pl.ds(0, len(OTHERS) * ROWS), :], kv_recv.at[a, j])
            for dx, dc in ARRIVAL[1:]:
                source = partner(s, dx, dc)
                if (a, j) == (V, 0):
                    kv_copy(V, 0, s, source).wait_recv()
                pass_on(a, j, source)

    @pl.when(jnp.logical_not(has_before))
    def _():
        kv_all[:, :, pl.ds(0, HALO), :] = jnp.zeros((2, SLOTS, HALO, HD), BF16)

    @pl.when(jnp.logical_not(has_after))
    def _():
        kv_all[:, :, pl.ds(HALO + GROUP, HALO), :] = jnp.zeros((2, SLOTS, HALO, HD), BF16)

    lane = lax.broadcasted_iota(jnp.int32, (8, HD), 1)
    ints[...] = jnp.zeros_like(ints)
    ints[0, :, :SAMPLES] = jnp.broadcast_to(image_buf[...] + TXT, (8, SAMPLES))
    ints[1, :, :SAMPLES] = jnp.broadcast_to(text_buf[...], (8, SAMPLES))
    lengths = ints[0]
    ends = lengths
    step = 1
    while step < SAMPLES:
        ends = ends + jnp.where(lane >= step, pltpu.roll(ends, step, 1), 0)
        step *= 2
    starts = (ends - lengths)[:1]
    ends = ends[:1]
    text_ends = starts + ints[1][:1]

    def mark(i, carry):
        first = pl.multiple_of(i * 64, 64)
        position = dp * GROUP - HALO + first + lax.broadcasted_iota(jnp.int32, (64, HD), 0)
        inside = (position >= starts) & (position < ends)
        usable = inside & ((position >= starts + TXT) | (position < text_ends))
        mark_k[pl.ds(first, 64), :] = jnp.where(usable, MARK_K, 0.0).astype(BF16)

        @pl.when((i >= HALO // 64) & (i < (HALO + GROUP) // 64))
        def _():
            mark_q[pl.ds(pl.multiple_of(first - HALO, 64), 64), :] = jnp.where(inside, MARK_Q, 0.0).astype(BF16)

        return carry

    lax.fori_loop(0, EXT // 64, mark, 0)

    own_rows = block(s * ROWS)
    own_ext = block(HALO + s * ROWS)
    wait_all(kv_all.at[K, :, own_ext, :], own_sem.at[0])
    wait_all(kv_all.at[V, :, own_ext, :], own_sem.at[1])
    wait_all(q_all.at[:, own_rows, :], own_sem.at[2])
    for j in range(SLOTS):
        attend(j)

    sent = k_src.at[:, pl.ds(0, len(OTHERS) * SLOTS * HD)]
    for i in range(3):
        wait_all(sent, x_send.at[i])

    @pl.when(has_after)
    def _():
        wait_all(kv_all.at[:, :, pl.ds(0, HALO), :], z_send.at[0])

    @pl.when(has_before)
    def _():
        wait_all(kv_all.at[:, :, pl.ds(0, HALO), :], z_send.at[1])

    wait_all(o_buf.at[:, own_rows, :], own_sem.at[3])
    for j in range(SLOTS):
        wait_all(out.at[:, pl.ds(0, len(OTHERS) * HD)], out_recv.at[j])
    wait_all(sent, x_send.at[3])


def solution(mesh):
    groups = mesh.shape["dp"]
    dma = pltpu.SemaphoreType.DMA

    def local(q_in, k_in, v_in, q_gain, k_gain, image_tokens, text_tokens):
        rows, width = q_in.shape
        return pl.pallas_call(
            functools.partial(kernel, groups),
            out_shape=jax.ShapeDtypeStruct((rows, width), BF16),
            in_specs=[pl.BlockSpec(memory_space=pltpu.HBM)] * 7,
            out_specs=pl.BlockSpec(memory_space=pl.ANY),
            scratch_shapes=[
                pltpu.VMEM((rows, width), BF16),
                pltpu.VMEM((rows, width), BF16),
                pltpu.VMEM((rows, width), BF16),
                pltpu.VMEM((rows, width), BF16),
                pltpu.VMEM((2, SLOTS, EXT, HD), BF16),
                pltpu.VMEM((SLOTS, GROUP, HD), BF16),
                pltpu.VMEM((SLOTS, GROUP, HD), BF16),
                pltpu.VMEM((GROUP, HD), BF16),
                pltpu.VMEM((EXT, HD), BF16),
                pltpu.VMEM((2, 1, HD), F32),
                pltpu.VMEM((1, SAMPLES), jnp.int32),
                pltpu.VMEM((1, SAMPLES), jnp.int32),
                pltpu.VMEM((2, 8, HD), jnp.int32),
                dma((6,)),
                dma((4,)),
                pltpu.SemaphoreType.REGULAR,
                dma((4,)),
                dma((2,)),
                dma((SEQ,)),
                dma((2, SLOTS)),
                dma((SLOTS,)),
                dma((SLOTS,)),
                dma((SLOTS,)),
                dma((SLOTS,)),
            ],
            compiler_params=pltpu.CompilerParams(
                collective_id=0, has_side_effects=True, vmem_limit_bytes=VMEM_BYTES
            ),
            cost_estimate=pl.CostEstimate(flops=4_000_000_000, bytes_accessed=4_000_000, transcendentals=5_000_000),
            name="joint_attention",
        )(
            q_in, k_in, v_in,
            q_gain.reshape(1, HD), k_gain.reshape(1, HD),
            image_tokens.reshape(1, SAMPLES), text_tokens.reshape(1, SAMPLES),
        )

    split = P(("dp", "seq"), None)
    return jax.shard_map(
        local,
        mesh=mesh,
        in_specs=(split, split, split, P(), P(), P(), P()),
        out_specs=split,
        check_vma=False,
    )
```

time: 56.7 us -> 47.5 us (0.84)
  the two profiles are of different devices: /device:TPU:1 before, /device:TPU:29 now
where the time goes in v2:
time: 47.5 us; the launch traced here: 47.4 us
  Pallas kernels  45.8 us (96%)
  local copies, waits for them, and re-layouts  1.57 us (3%)
    pallas_call x1, Pallas kernels, local(): pl.pallas_call(functools.partial(kernel, groups), out_shape=jax.ShapeDtyp...  45.8 us
    unnamed x9, local copies, waits for them, and re-layouts  1.57 us

profile of v2, /device:TPU:29, one launch (start us, length us, event | category | flops | bytes accessed | tf_op | source)
XLA Modules:
  0.0 47.4 jit_solution(7333213080234479177)
XLA Ops:
  0.0 0.0 copy-start.3
  0.0 0.0 copy-start
  0.0 0.0 copy-start.1
  0.0 0.0 copy-start.2
  0.0 0.6 %copy-done.3 = s32[64]{0:T(128)S(1)} copy-done((s32[64]{0:T(128)S(1)}, s32[64]{0:T(128)}, u32[]{:S(2)}) %copy-start.3) | copy-done | bytes 280
  0.7 0.0 copy-done
  0.7 0.0 copy-done.1
  0.7 0.0 copy-done.2
  0.7 45.8 %joint_attention.1 = bf16[128,3072]{1,0:T(8,128)(2,1)S(1)} custom-call(bf16[128,3072]{1,0:T(8,128)(2,1)} %q_in.1, bf16[128,3072]{1,0:T(8,128)(2,1)} %k_in.1, bf16[128,3072]{1,0:T(8,128)(2,1)} %v_in.1, f32[1,128]{1,0:T(1,128)S(1)} %bitcast.4, f32[1,128]{1,0:T(1,128)S(1)} %bitcast.5, s32[1,64]{1,0:T(1,128)S(1)} %bitcast.6, s32[1,64]{1,0:T(1,128)S(1)} %bitcast.7), custom_call_target="tpu_custom_call" | custom-call | flops 4000000000 | bytes 4000000 | tf_op jit(solution)/shard_map/joint_attention/pallas_call | solution.py:351
  46.5 0.9 %copy.9 = bf16[128,3072]{1,0:T(8,128)(2,1)} copy(bf16[128,3072]{1,0:T(8,128)(2,1)S(1)} %joint_attention.1) | data formatting | bytes 1572864
Async XLA Ops:
  0.0 0.7 %copy-start.3 = (s32[64]{0:T(128)S(1)}, s32[64]{0:T(128)}, u32[]{:S(2)}) copy-start(s32[64]{0:T(128)} %param.13) | copy-start | bytes 772
  0.0 0.7 %copy-start = (f32[128]{0:T(128)S(1)}, f32[128]{0:T(128)}, u32[]{:S(2)}) copy-start(f32[128]{0:T(128)} %param.10) | copy-start | bytes 1540
  0.0 0.7 %copy-start.1 = (f32[128]{0:T(128)S(1)}, f32[128]{0:T(128)}, u32[]{:S(2)}) copy-start(f32[128]{0:T(128)} %param.11) | copy-start | bytes 1540
  0.0 0.7 %copy-start.2 = (s32[64]{0:T(128)S(1)}, s32[64]{0:T(128)}, u32[]{:S(2)}) copy-start(s32[64]{0:T(128)} %param.12) | copy-start | bytes 772

commit v3 on v2

--- a/solution.py
+++ b/solution.py
@@ -25,14 +25,17 @@
 SAMPLES = 64
 VMEM_BYTES = 53 * 1024 * 1024
 NORM_HEADS = 12
-K, V = 0, 1
+K, V, Q = 0, 1, 2
+NEAR, FAR = 0, 1
+ORDER = ((V, 0), (K, 0), (V, 1), (K, 1), (V, 2), (K, 2), (Q, 0), (Q, 1), (Q, 2))
+AHEAD = 4
 
 MARK_Q = 64.0
 MARK_K = 128.0
 SCALE = 1.4426950408889634 / HD**0.5
 
-OTHERS = ((1, 0), (1, 1), (-1, 0), (-1, 1), (2, 0), (2, 1), (0, 1))
-ARRIVAL = ((0, 0), (0, 1), (1, 0), (-1, 0), (1, 1), (-1, 1), (2, 0), (2, 1))
+OTHERS = ((1, 0), (-1, 0), (2, 0), (1, 1), (-1, 1), (2, 1), (0, 1))
+ARRIVAL = ((0, 1), (1, 0), (-1, 0), (1, 1), (-1, 1), (2, 0), (2, 1))
 NT = (((1,), (1,)), ((), ()))
 
 
@@ -123,38 +126,45 @@
                 return source_of(a).at[pl.ds(first, count), cols(s * SLOTS + j)]
             return kv_all.at[a, j, block(HALO + source * ROWS + first, count), :]
 
-        def to_after(first, count):
+        def to_after(first, count, sem):
             remote(
                 rows(first, count), kv_all.at[a, j, block(source * ROWS + first - (GROUP - HALO), count), :],
-                z_send.at[0], halo_left.at[j], (after, s),
+                z_send.at[0], sem, (after, s),
             ).start()
 
-        def to_before(count):
+        def to_before(count, sem):
             remote(
                 rows(0, count), kv_all.at[a, j, block(HALO + GROUP + source * ROWS, count), :],
-                z_send.at[1], halo_right.at[j], (before, s),
+                z_send.at[1], sem, (before, s),
             ).start()
 
-        @pl.when((source >= 3) & has_after)
-        def _():
-            to_after(0, ROWS)
+        @pl.when((source >= 6) & has_after)
+        def _():
+            to_after(0, ROWS, halo_left.at[NEAR, j])
+
+        @pl.when((source >= 3) & (source < 6) & has_after)
+        def _():
+            to_after(0, ROWS, halo_left.at[FAR, j])
 
         @pl.when((source == 2) & has_after)
         def _():
-            to_after(64, ROWS - 64)
-
-        @pl.when((source <= 4) & has_before)
-        def _():
-            to_before(ROWS)
+            to_after(64, ROWS - 64, halo_left.at[FAR, j])
+
+        @pl.when((source < 2) & has_before)
+        def _():
+            to_before(ROWS, halo_right.at[NEAR, j])
+
+        @pl.when((source >= 2) & (source <= 4) & has_before)
+        def _():
+            to_before(ROWS, halo_right.at[FAR, j])
 
         @pl.when((source == 5) & has_before)
         def _():
-            to_before(64)
-
-    def pass_own():
+            to_before(64, halo_right.at[FAR, j])
+
+    def pass_own(a):
         for j in range(SLOTS):
-            for a in (V, K):
-                pass_on(a, j, s, own=True)
+            pass_on(a, j, s, own=True)
 
     def own_kv(a, j):
         return pltpu.make_async_copy(
@@ -182,19 +192,19 @@
 
         lax.fori_loop(0, SEQ * SLOTS // NORM_HEADS, some, 0)
 
-    def attend(j):
-        wait_all(q_all.at[0, pl.ds(0, len(OTHERS) * ROWS), :], q_recv.at[j])
-
-        @pl.when(has_before)
-        def _():
-            wait_all(kv_all.at[K, 0, pl.ds(0, 2 * HALO), :], halo_left.at[j])
-
-        @pl.when(has_after)
-        def _():
-            wait_all(kv_all.at[K, 0, pl.ds(0, 2 * HALO), :], halo_right.at[j])
-
-        for i in range(GROUP // BLOCK):
-            rows, window = pl.ds(i * BLOCK, BLOCK), pl.ds(i * BLOCK, WINDOW)
+    def wait_halo(sems, part, j, present):
+        count = 2 * (2 * ROWS if part == NEAR else HALO - 2 * ROWS)
+
+        @pl.when(present)
+        def _():
+            wait_all(kv_all.at[K, 0, pl.ds(0, count), :], sems.at[part, j])
+
+    def attend(j, first, blocks):
+        for i in range(blocks):
+            start = first + i * BLOCK
+            if not isinstance(start, int):
+                start = pl.multiple_of(start, BLOCK)
+            rows, window = pl.ds(start, BLOCK), pl.ds(start, WINDOW)
             q = jnp.concatenate([q_all[j, rows, :], mark_q[rows, :]], axis=1)
             k = jnp.concatenate([kv_all[K, j, window, :], mark_k[window, :]], axis=1)
             v = kv_all[V, j, window, :]
@@ -203,58 +213,88 @@
             weights = jnp.exp2((scores - top) * SCALE).astype(BF16)
             sums = jnp.dot(weights, jnp.concatenate([v, jnp.ones_like(v)], axis=1), preferred_element_type=F32)
             o_buf[j, rows, :] = (sums[:, :HD] / sums[:, HD:]).astype(BF16)
+
+    def attend_whole(j):
+        wait_all(q_all.at[0, pl.ds(0, len(OTHERS) * ROWS), :], q_recv.at[j])
+        for part in (NEAR, FAR):
+            wait_halo(halo_left, part, j, has_before)
+            wait_halo(halo_right, part, j, has_after)
+        attend(j, 0, GROUP // BLOCK)
         for dx, dc in OTHERS:
             out_copy(j, partner(s, dx, dc), s).start()
         own_out(j).start()
+
+    def attend_halves(j):
+        wait_all(q_all.at[0, pl.ds(0, len(OTHERS) * ROWS), :], q_recv.at[j])
+        wait_halo(halo_left, NEAR, j, has_before)
+        wait_halo(halo_right, NEAR, j, has_after)
+        place = lax.rem(dp, 8)
+        left_late = (place == 0) | (place == 7) | (s < 4)
+        for upper in (left_late, jnp.logical_not(left_late)):
+            wait_halo(halo_right, FAR, j, upper & has_after)
+            wait_halo(halo_left, FAR, j, jnp.logical_not(upper) & has_before)
+            half = jnp.where(upper, 1, 0)
+            attend(j, half * (GROUP // 2), GROUP // 2 // BLOCK)
+            for i in range(SEQ // 2):
+                to = half * (SEQ // 2) + i
+
+                @pl.when(to != s)
+                def _():
+                    out_copy(j, to, s).start()
+
+                @pl.when(to == s)
+                def _():
+                    own_out(j).start()
+
+    @pl.when(even)
+    def _():
+        pl.semaphore_wait(barrier, len(OTHERS))
+
+    @pl.when(odd & has_after)
+    def _():
+        pl.semaphore_wait(barrier, len(OTHERS) + 2)
+
+    @pl.when(odd & jnp.logical_not(has_after))
+    def _():
+        pl.semaphore_wait(barrier, len(OTHERS) + 1)
+
+    def send(a, j):
+        for dx, dc in OTHERS:
+            to = partner(s, dx, dc)
+            (q_copy(j, to, s) if a == Q else kv_copy(a, j, to, s)).start()
+
+    send(V, 0)
+
+    @pl.when(odd)
+    def _():
+        pl.semaphore_signal(ready, 1, device_id=(before, s), device_id_type=MESH)
+
+    @pl.when(odd & has_after)
+    def _():
+        pl.semaphore_signal(ready, 1, device_id=(after, s), device_id_type=MESH)
+
+    @pl.when(odd)
+    def _():
+        pass_own(V)
 
     load_k.wait()
     for copy in small:
         copy.wait()
     normalize(k_buf, gains[0], k_src)
-
-    @pl.when(even)
-    def _():
-        pl.semaphore_wait(barrier, len(OTHERS))
-
-    @pl.when(odd & has_after)
-    def _():
-        pl.semaphore_wait(barrier, len(OTHERS) + 2)
-
-    @pl.when(odd & jnp.logical_not(has_after))
-    def _():
-        pl.semaphore_wait(barrier, len(OTHERS) + 1)
-
-    def send_kv(a, j):
-        for dx, dc in OTHERS:
-            kv_copy(a, j, partner(s, dx, dc), s).start()
-
-    send_kv(V, 0)
+    send(K, 0)
 
     @pl.when(odd)
     def _():
-        pl.semaphore_signal(ready, 1, device_id=(before, s), device_id_type=MESH)
-
-    @pl.when(odd & has_after)
-    def _():
-        pl.semaphore_signal(ready, 1, device_id=(after, s), device_id_type=MESH)
-
-    send_kv(K, 0)
-
-    @pl.when(odd)
-    def _():
-        pass_own()
-
-    for j in range(1, SLOTS):
-        send_kv(V, j)
-        send_kv(K, j)
+        pass_own(K)
+
+    for a, j in ORDER[2:AHEAD]:
+        send(a, j)
     for j in range(SLOTS):
         own_kv(K, j).start()
         own_kv(V, j).start()
     load_q.wait()
     normalize(q_buf, gains[1], q_src)
     for j in range(SLOTS):
-        for dx, dc in OTHERS:
-            q_copy(j, partner(s, dx, dc), s).start()
         own_q(j).start()
 
     @pl.when(even & has_after & has_before)
@@ -267,17 +307,19 @@
 
     @pl.when(even)
     def _():
-        pass_own()
-
-    for j in range(SLOTS):
-        for a in (V, K):
-            if (a, j) != (V, 0):
-                wait_all(kv_all.at[a, 0, pl.ds(0, len(OTHERS) * ROWS), :], kv_recv.at[a, j])
-            for dx, dc in ARRIVAL[1:]:
-                source = partner(s, dx, dc)
-                if (a, j) == (V, 0):
-                    kv_copy(V, 0, s, source).wait_recv()
-                pass_on(a, j, source)
+        pass_own(V)
+        pass_own(K)
+
+    for at, (a, j) in enumerate(ORDER[:6]):
+        if at > 0:
+            wait_all(kv_all.at[a, 0, pl.ds(0, len(OTHERS) * ROWS), :], kv_recv.at[a, j])
+        for dx, dc in ARRIVAL:
+            source = partner(s, dx, dc)
+            if at == 0:
+                kv_copy(a, j, s, source).wait_recv()
+            pass_on(a, j, source)
+        if at + AHEAD < len(ORDER):
+            send(*ORDER[at + AHEAD])
 
     @pl.when(jnp.logical_not(has_before))
     def _():
@@ -321,8 +363,9 @@
     wait_all(kv_all.at[K, :, own_ext, :], own_sem.at[0])
     wait_all(kv_all.at[V, :, own_ext, :], own_sem.at[1])
     wait_all(q_all.at[:, own_rows, :], own_sem.at[2])
-    for j in range(SLOTS):
-        attend(j)
+    for j in range(SLOTS - 1):
+        attend_whole(j)
+    attend_halves(SLOTS - 1)
 
     sent = k_src.at[:, pl.ds(0, len(OTHERS) * SLOTS * HD)]
     for i in range(3):
@@ -375,8 +418,8 @@
                 dma((SEQ,)),
                 dma((2, SLOTS)),
                 dma((SLOTS,)),
-                dma((SLOTS,)),
-                dma((SLOTS,)),
+                dma((2, SLOTS)),
+                dma((2, SLOTS)),
                 dma((SLOTS,)),
             ],
             compiler_params=pltpu.CompilerParams(

time: 47.5 us -> 45.2 us (0.952)
  the two profiles are of different devices: /device:TPU:29 before, /device:TPU:1 now
where the time goes in v3:
time: 45.2 us; the launch traced here: 44.6 us
  Pallas kernels  43 us (95%)
  local copies, waits for them, and re-layouts  1.57 us (3%)
    pallas_call x1, Pallas kernels, local(): pl.pallas_call(functools.partial(kernel, groups), out_shape=jax.ShapeDtyp...  43 us
    unnamed x9, local copies, waits for them, and re-layouts  1.57 us

profile of v3, /device:TPU:1, one launch (start us, length us, event | category | flops | bytes accessed | tf_op | source)
XLA Modules:
  0.0 44.6 jit_solution(1559413309269206000)
XLA Ops:
  0.0 0.0 copy-start.3
  0.0 0.0 copy-start
  0.0 0.0 copy-start.1
  0.0 0.0 copy-start.2
  0.0 0.6 %copy-done.3 = s32[64]{0:T(128)S(1)} copy-done((s32[64]{0:T(128)S(1)}, s32[64]{0:T(128)}, u32[]{:S(2)}) %copy-start.3) | copy-done | bytes 280
  0.7 0.0 copy-done
  0.7 0.0 copy-done.1
  0.7 0.0 copy-done.2
  0.7 43.0 %joint_attention.1 = bf16[128,3072]{1,0:T(8,128)(2,1)S(1)} custom-call(bf16[128,3072]{1,0:T(8,128)(2,1)} %q_in.1, bf16[128,3072]{1,0:T(8,128)(2,1)} %k_in.1, bf16[128,3072]{1,0:T(8,128)(2,1)} %v_in.1, f32[1,128]{1,0:T(1,128)S(1)} %bitcast.4, f32[1,128]{1,0:T(1,128)S(1)} %bitcast.5, s32[1,64]{1,0:T(1,128)S(1)} %bitcast.6, s32[1,64]{1,0:T(1,128)S(1)} %bitcast.7), custom_call_target="tpu_custom_call" | custom-call | flops 4000000000 | bytes 4000000 | tf_op jit(solution)/shard_map/joint_attention/pallas_call | solution.py:394
  43.7 0.9 %copy.9 = bf16[128,3072]{1,0:T(8,128)(2,1)} copy(bf16[128,3072]{1,0:T(8,128)(2,1)S(1)} %joint_attention.1) | data formatting | bytes 1572864
Async XLA Ops:
  0.0 0.7 %copy-start.3 = (s32[64]{0:T(128)S(1)}, s32[64]{0:T(128)}, u32[]{:S(2)}) copy-start(s32[64]{0:T(128)} %param.13) | copy-start | bytes 772
  0.0 0.7 %copy-start = (f32[128]{0:T(128)S(1)}, f32[128]{0:T(128)}, u32[]{:S(2)}) copy-start(f32[128]{0:T(128)} %param.10) | copy-start | bytes 1540
  0.0 0.7 %copy-start.1 = (f32[128]{0:T(128)S(1)}, f32[128]{0:T(128)}, u32[]{:S(2)}) copy-start(f32[128]{0:T(128)} %param.11) | copy-start | bytes 1540
  0.0 0.7 %copy-start.2 = (s32[64]{0:T(128)S(1)}, s32[64]{0:T(128)}, u32[]{:S(2)}) copy-start(s32[64]{0:T(128)} %param.12) | copy-start | bytes 772

commit v4 on v3

--- a/solution.py
+++ b/solution.py
@@ -23,10 +23,10 @@
 BLOCK = 256
 WINDOW = BLOCK + 2 * HALO
 SAMPLES = 64
-VMEM_BYTES = 53 * 1024 * 1024
+VMEM_BYTES = 48 * 1024 * 1024
 NORM_HEADS = 12
 K, V, Q = 0, 1, 2
-NEAR, FAR = 0, 1
+PARTS = 3
 ORDER = ((V, 0), (K, 0), (V, 1), (K, 1), (V, 2), (K, 2), (Q, 0), (Q, 1), (Q, 2))
 AHEAD = 4
 
@@ -120,51 +120,59 @@
             x_send.at[3], out_recv.at[j], (dp, to),
         )
 
-    def pass_on(a, j, source, own=False):
-        def rows(first, count):
-            if own:
-                return source_of(a).at[pl.ds(first, count), cols(s * SLOTS + j)]
-            return kv_all.at[a, j, block(HALO + source * ROWS + first, count), :]
-
-        def to_after(first, count, sem):
+    def halo_rows(a, j, source, first, count, own):
+        if own:
+            return source_of(a).at[pl.ds(first, count), cols(s * SLOTS + j)]
+        return kv_all.at[a, j, block(HALO + source * ROWS + first, count), :]
+
+    def pass_after(a, j, source, own=False):
+        def start(first):
             remote(
-                rows(first, count), kv_all.at[a, j, block(source * ROWS + first - (GROUP - HALO), count), :],
-                z_send.at[0], sem, (after, s),
+                halo_rows(a, j, source, first, ROWS - first, own),
+                kv_all.at[a, j, block(source * ROWS + first - (GROUP - HALO), ROWS - first), :],
+                z_send.at[0], halo_left.at[(SEQ - 1 - source) // 2, j], (after, s),
             ).start()
 
-        def to_before(count, sem):
+        @pl.when((source >= 3) & has_after)
+        def _():
+            start(0)
+
+        @pl.when((source == 2) & has_after)
+        def _():
+            start(64)
+
+    def pass_before(a, j, source, own=False):
+        def start(count):
             remote(
-                rows(0, count), kv_all.at[a, j, block(HALO + GROUP + source * ROWS, count), :],
-                z_send.at[1], sem, (before, s),
+                halo_rows(a, j, source, 0, count, own),
+                kv_all.at[a, j, block(HALO + GROUP + source * ROWS, count), :],
+                z_send.at[1], halo_right.at[source // 2, j], (before, s),
             ).start()
 
-        @pl.when((source >= 6) & has_after)
-        def _():
-            to_after(0, ROWS, halo_left.at[NEAR, j])
-
-        @pl.when((source >= 3) & (source < 6) & has_after)
-        def _():
-            to_after(0, ROWS, halo_left.at[FAR, j])
-
-        @pl.when((source == 2) & has_after)
-        def _():
-            to_after(64, ROWS - 64, halo_left.at[FAR, j])
-
-        @pl.when((source < 2) & has_before)
-        def _():
-            to_before(ROWS, halo_right.at[NEAR, j])
-
-        @pl.when((source >= 2) & (source <= 4) & has_before)
-        def _():
-            to_before(ROWS, halo_right.at[FAR, j])
+        @pl.when((source <= 4) & has_before)
+        def _():
+            start(ROWS)
 
         @pl.when((source == 5) & has_before)
         def _():
-            to_before(64, halo_right.at[FAR, j])
+            start(64)
 
     def pass_own(a):
         for j in range(SLOTS):
-            pass_on(a, j, s, own=True)
+            pass_after(a, j, s, own=True)
+            pass_before(a, j, s, own=True)
+
+    def pass_part(a, j, part):
+        for source in (2 * part, 2 * part + 1):
+            mirror = SEQ - 1 - source
+
+            @pl.when(mirror != s)
+            def _():
+                pass_after(a, j, mirror)
+
+            @pl.when(source != s)
+            def _():
+                pass_before(a, j, source)
 
     def own_kv(a, j):
         return pltpu.make_async_copy(
@@ -193,7 +201,7 @@
         lax.fori_loop(0, SEQ * SLOTS // NORM_HEADS, some, 0)
 
     def wait_halo(sems, part, j, present):
-        count = 2 * (2 * ROWS if part == NEAR else HALO - 2 * ROWS)
+        count = 2 * min(2 * ROWS, HALO - part * 2 * ROWS)
 
         @pl.when(present)
         def _():
@@ -216,7 +224,7 @@
 
     def attend_whole(j):
         wait_all(q_all.at[0, pl.ds(0, len(OTHERS) * ROWS), :], q_recv.at[j])
-        for part in (NEAR, FAR):
+        for part in range(PARTS):
             wait_halo(halo_left, part, j, has_before)
             wait_halo(halo_right, part, j, has_after)
         attend(j, 0, GROUP // BLOCK)
@@ -224,19 +232,23 @@
             out_copy(j, partner(s, dx, dc), s).start()
         own_out(j).start()
 
-    def attend_halves(j):
+    def attend_steps(j):
         wait_all(q_all.at[0, pl.ds(0, len(OTHERS) * ROWS), :], q_recv.at[j])
-        wait_halo(halo_left, NEAR, j, has_before)
-        wait_halo(halo_right, NEAR, j, has_after)
-        place = lax.rem(dp, 8)
-        left_late = (place == 0) | (place == 7) | (s < 4)
-        for upper in (left_late, jnp.logical_not(left_late)):
-            wait_halo(halo_right, FAR, j, upper & has_after)
-            wait_halo(halo_left, FAR, j, jnp.logical_not(upper) & has_before)
-            half = jnp.where(upper, 1, 0)
-            attend(j, half * (GROUP // 2), GROUP // 2 // BLOCK)
-            for i in range(SEQ // 2):
-                to = half * (SEQ // 2) + i
+        wait_halo(halo_left, 0, j, has_before)
+        wait_halo(halo_right, 0, j, has_after)
+        left_late = s < SEQ // 2
+        right_late = jnp.logical_not(left_late)
+        for part in range(1, PARTS):
+            wait_halo(halo_right, part, j, left_late & has_after)
+            wait_halo(halo_left, part, j, right_late & has_before)
+        for part, (upward, downward, blocks) in enumerate(((2, 0, 2), (1, 2, 1), (0, 3, 1))):
+            if part > 0:
+                wait_halo(halo_left, part, j, left_late & has_before)
+                wait_halo(halo_right, part, j, right_late & has_after)
+            first = jnp.where(left_late, upward, downward)
+            attend(j, first * BLOCK, blocks)
+            for i in range(blocks * BLOCK // ROWS):
+                to = first * (BLOCK // ROWS) + i
 
                 @pl.when(to != s)
                 def _():
@@ -313,11 +325,19 @@
     for at, (a, j) in enumerate(ORDER[:6]):
         if at > 0:
             wait_all(kv_all.at[a, 0, pl.ds(0, len(OTHERS) * ROWS), :], kv_recv.at[a, j])
-        for dx, dc in ARRIVAL:
-            source = partner(s, dx, dc)
-            if at == 0:
-                kv_copy(a, j, s, source).wait_recv()
-            pass_on(a, j, source)
+        if j == SLOTS - 1:
+            pass_part(a, j, 0)
+            if a == K:
+                for part in range(1, PARTS):
+                    pass_part(V, j, part)
+                    pass_part(K, j, part)
+        else:
+            for dx, dc in ARRIVAL:
+                source = partner(s, dx, dc)
+                if at == 0:
+                    kv_copy(a, j, s, source).wait_recv()
+                pass_after(a, j, source)
+                pass_before(a, j, source)
         if at + AHEAD < len(ORDER):
             send(*ORDER[at + AHEAD])
 
@@ -365,7 +385,7 @@
     wait_all(q_all.at[:, own_rows, :], own_sem.at[2])
     for j in range(SLOTS - 1):
         attend_whole(j)
-    attend_halves(SLOTS - 1)
+    attend_steps(SLOTS - 1)
 
     sent = k_src.at[:, pl.ds(0, len(OTHERS) * SLOTS * HD)]
     for i in range(3):
@@ -391,6 +411,11 @@
 
     def local(q_in, k_in, v_in, q_gain, k_gain, image_tokens, text_tokens):
         rows, width = q_in.shape
+        operands = (
+            q_in, k_in, v_in,
+            q_gain.reshape(1, HD), k_gain.reshape(1, HD),
+            image_tokens.reshape(1, SAMPLES), text_tokens.reshape(1, SAMPLES),
+        )
         return pl.pallas_call(
             functools.partial(kernel, groups),
             out_shape=jax.ShapeDtypeStruct((rows, width), BF16),
@@ -418,8 +443,8 @@
                 dma((SEQ,)),
                 dma((2, SLOTS)),
                 dma((SLOTS,)),
-                dma((2, SLOTS)),
-                dma((2, SLOTS)),
+                dma((PARTS, SLOTS)),
+                dma((PARTS, SLOTS)),
                 dma((SLOTS,)),
             ],
             compiler_params=pltpu.CompilerParams(
@@ -427,11 +452,7 @@
             ),
             cost_estimate=pl.CostEstimate(flops=4_000_000_000, bytes_accessed=4_000_000, transcendentals=5_000_000),
             name="joint_attention",
-        )(
-            q_in, k_in, v_in,
-            q_gain.reshape(1, HD), k_gain.reshape(1, HD),
-            image_tokens.reshape(1, SAMPLES), text_tokens.reshape(1, SAMPLES),
-        )
+        )(*[pltpu.with_memory_space_constraint(operand, pltpu.HBM) for operand in operands])
 
     split = P(("dp", "seq"), None)
     return jax.shard_map(

time: 45.2 us -> 43.4 us (0.960)
  the two profiles are of different devices: /device:TPU:1 before, /device:TPU:25 now
where the time goes in v4:
time: 43.4 us; the launch traced here: 43.3 us
  Pallas kernels  42.4 us (98%)
  local copies, waits for them, and re-layouts  0.88 us (2%)
    pallas_call x1, Pallas kernels, local(): pl.pallas_call(functools.partial(kernel, groups), out_shape=jax.ShapeDtyp...  42.4 us
    unnamed x1, local copies, waits for them, and re-layouts  0.88 us

profile of v4, /device:TPU:25, one launch (start us, length us, event | category | flops | bytes accessed | tf_op | source)
XLA Modules:
  0.0 43.3 jit_solution(6878658003509718689)
XLA Ops:
  0.0 42.4 %joint_attention.1 = bf16[128,3072]{1,0:T(8,128)(2,1)S(1)} custom-call(bf16[128,3072]{1,0:T(8,128)(2,1)} %q_in.1, bf16[128,3072]{1,0:T(8,128)(2,1)} %k_in.1, bf16[128,3072]{1,0:T(8,128)(2,1)} %v_in.1, f32[1,128]{1,0:T(1,128)} %bitcast.4, f32[1,128]{1,0:T(1,128)} %bitcast.5, s32[1,64]{1,0:T(1,128)} %bitcast.6, s32[1,64]{1,0:T(1,128)} %bitcast.7), custom_call_target="tpu_custom_call" | custom-call | flops 4000000000 | bytes 4000000 | tf_op jit(solution)/shard_map/joint_attention/pallas_call | solution.py:419
  42.4 0.9 %copy.9 = bf16[128,3072]{1,0:T(8,128)(2,1)} copy(bf16[128,3072]{1,0:T(8,128)(2,1)S(1)} %joint_attention.1) | data formatting | bytes 1572864

commit v5 on v4

--- a/solution.py
+++ b/solution.py
@@ -207,20 +207,25 @@
         def _():
             wait_all(kv_all.at[K, 0, pl.ds(0, count), :], sems.at[part, j])
 
+    def weigh(j, rows, keys):
+        q = jnp.concatenate([q_all[j, rows, :], mark_q[rows, :]], axis=1)
+        k = jnp.concatenate([kv_all[K, j, keys, :], mark_k[keys, :]], axis=1)
+        v = kv_all[V, j, keys, :]
+        scores = lax.dot_general(q, k, NT, preferred_element_type=F32)
+        top = jnp.max(scores, axis=1, keepdims=True)
+        weights = jnp.exp2((scores - top) * SCALE).astype(BF16)
+        return top, jnp.dot(weights, jnp.concatenate([v, jnp.ones_like(v)], axis=1), preferred_element_type=F32)
+
+    def keep(j, rows, sums):
+        o_buf[j, rows, :] = (sums[:, :HD] / sums[:, HD:]).astype(BF16)
+
+    def part_of(first, count):
+        return pl.ds(first if isinstance(first, int) else pl.multiple_of(first, HD), count)
+
     def attend(j, first, blocks):
         for i in range(blocks):
-            start = first + i * BLOCK
-            if not isinstance(start, int):
-                start = pl.multiple_of(start, BLOCK)
-            rows, window = pl.ds(start, BLOCK), pl.ds(start, WINDOW)
-            q = jnp.concatenate([q_all[j, rows, :], mark_q[rows, :]], axis=1)
-            k = jnp.concatenate([kv_all[K, j, window, :], mark_k[window, :]], axis=1)
-            v = kv_all[V, j, window, :]
-            scores = lax.dot_general(q, k, NT, preferred_element_type=F32)
-            top = jnp.max(scores, axis=1, keepdims=True)
-            weights = jnp.exp2((scores - top) * SCALE).astype(BF16)
-            sums = jnp.dot(weights, jnp.concatenate([v, jnp.ones_like(v)], axis=1), preferred_element_type=F32)
-            o_buf[j, rows, :] = (sums[:, :HD] / sums[:, HD:]).astype(BF16)
+            rows = part_of(first + i * BLOCK, BLOCK)
+            keep(j, rows, weigh(j, rows, part_of(first + i * BLOCK, WINDOW))[1])
 
     def attend_whole(j):
         wait_all(q_all.at[0, pl.ds(0, len(OTHERS) * ROWS), :], q_recv.at[j])
@@ -236,27 +241,43 @@
         wait_all(q_all.at[0, pl.ds(0, len(OTHERS) * ROWS), :], q_recv.at[j])
         wait_halo(halo_left, 0, j, has_before)
         wait_halo(halo_right, 0, j, has_after)
-        left_late = s < SEQ // 2
+        left_late = (s < SEQ // 2) | ((s < 6) & (lax.rem(dp, 8) == 0) & has_before)
         right_late = jnp.logical_not(left_late)
+
+        def send_rows(first, count):
+            for i in range(count // ROWS):
+                to = first // ROWS + i
+
+                @pl.when(to != s)
+                def _():
+                    out_copy(j, to, s).start()
+
+                @pl.when(to == s)
+                def _():
+                    own_out(j).start()
+
         for part in range(1, PARTS):
             wait_halo(halo_right, part, j, left_late & has_after)
             wait_halo(halo_left, part, j, right_late & has_before)
-        for part, (upward, downward, blocks) in enumerate(((2, 0, 2), (1, 2, 1), (0, 3, 1))):
-            if part > 0:
-                wait_halo(halo_left, part, j, left_late & has_before)
-                wait_halo(halo_right, part, j, right_late & has_after)
-            first = jnp.where(left_late, upward, downward)
-            attend(j, first * BLOCK, blocks)
-            for i in range(blocks * BLOCK // ROWS):
-                to = first * (BLOCK // ROWS) + i
-
-                @pl.when(to != s)
-                def _():
-                    out_copy(j, to, s).start()
-
-                @pl.when(to == s)
-                def _():
-                    own_out(j).start()
+        half = jnp.where(left_late, 2 * BLOCK, 0)
+        attend(j, half, 2)
+        send_rows(half, 2 * BLOCK)
+
+        wait_halo(halo_left, 1, j, left_late & has_before)
+        wait_halo(halo_right, 1, j, right_late & has_after)
+        middle = jnp.where(left_late, BLOCK, 2 * BLOCK)
+        edge = part_of(jnp.where(left_late, 0, 3 * BLOCK), BLOCK)
+        attend(j, middle, 1)
+        top_near, sums_near = weigh(j, edge, part_of(jnp.where(left_late, BLOCK, 3 * BLOCK), WINDOW - BLOCK))
+        send_rows(middle, BLOCK)
+
+        wait_halo(halo_left, 2, j, left_late & has_before)
+        wait_halo(halo_right, 2, j, right_late & has_after)
+        top_far, sums_far = weigh(j, edge, part_of(jnp.where(left_late, 0, EXT - BLOCK), BLOCK))
+        top = jnp.maximum(top_near, top_far)
+        near, far = jnp.exp2((top_near - top) * SCALE), jnp.exp2((top_far - top) * SCALE)
+        keep(j, edge, sums_near * near + sums_far * far)
+        send_rows(jnp.where(left_late, 0, 3 * BLOCK), BLOCK)
 
     @pl.when(even)
     def _():

time: 43.4 us -> 42.8 us (0.986)
  the two profiles are of different devices: /device:TPU:25 before, /device:TPU:1 now
where the time goes in v5:
time: 42.8 us; the launch traced here: 42.3 us
  Pallas kernels  41.4 us (97%)
  local copies, waits for them, and re-layouts  0.88 us (2%)
    pallas_call x1, Pallas kernels, local(): pl.pallas_call(functools.partial(kernel, groups), out_shape=jax.ShapeDtyp...  41.4 us
    unnamed x1, local copies, waits for them, and re-layouts  0.88 us

profile of v5, /device:TPU:1, one launch (start us, length us, event | category | flops | bytes accessed | tf_op | source)
XLA Modules:
  0.0 42.3 jit_solution(14444060707977243672)
XLA Ops:
  0.0 41.4 %joint_attention.1 = bf16[128,3072]{1,0:T(8,128)(2,1)S(1)} custom-call(bf16[128,3072]{1,0:T(8,128)(2,1)} %q_in.1, bf16[128,3072]{1,0:T(8,128)(2,1)} %k_in.1, bf16[128,3072]{1,0:T(8,128)(2,1)} %v_in.1, f32[1,128]{1,0:T(1,128)} %bitcast.4, f32[1,128]{1,0:T(1,128)} %bitcast.5, s32[1,64]{1,0:T(1,128)} %bitcast.6, s32[1,64]{1,0:T(1,128)} %bitcast.7), custom_call_target="tpu_custom_call" | custom-call | flops 4000000000 | bytes 4000000 | tf_op jit(solution)/shard_map/joint_attention/pallas_call | solution.py:440
  41.4 0.9 %copy.9 = bf16[128,3072]{1,0:T(8,128)(2,1)} copy(bf16[128,3072]{1,0:T(8,128)(2,1)S(1)} %joint_attention.1) | data formatting | bytes 1572864

commit v6 on v5

--- a/solution.py
+++ b/solution.py
@@ -105,32 +105,35 @@
         recv = v_recv.at[source] if (a, j) == (V, 0) else kv_recv.at[a, j]
         return remote(
             source_of(a).at[:, cols(to * SLOTS + j)], kv_all.at[a, j, block(HALO + source * ROWS), :],
-            x_send.at[a], recv, (dp, to),
+            x_send, recv, (dp, to),
         )
 
     def q_copy(j, to, source):
         return remote(
             q_src.at[:, cols(to * SLOTS + j)], q_all.at[j, block(source * ROWS), :],
-            x_send.at[2], q_recv.at[j], (dp, to),
+            x_send, q_recv.at[j], (dp, to),
         )
 
     def out_copy(j, to, source):
         return remote(
             o_buf.at[j, block(to * ROWS), :], out.at[:, cols(source * SLOTS + j)],
-            x_send.at[3], out_recv.at[j], (dp, to),
+            x_send, out_recv, (dp, to),
         )
 
     def halo_rows(a, j, source, first, count, own):
         if own:
             return source_of(a).at[pl.ds(first, count), cols(s * SLOTS + j)]
         return kv_all.at[a, j, block(HALO + source * ROWS + first, count), :]
+
+    def halo_index(j, part):
+        return j + part if j == SLOTS - 1 else j
 
     def pass_after(a, j, source, own=False):
         def start(first):
             remote(
                 halo_rows(a, j, source, first, ROWS - first, own),
                 kv_all.at[a, j, block(source * ROWS + first - (GROUP - HALO), ROWS - first), :],
-                z_send.at[0], halo_left.at[(SEQ - 1 - source) // 2, j], (after, s),
+                z_send.at[0], halo_left.at[halo_index(j, (SEQ - 1 - source) // 2)], (after, s),
             ).start()
 
         @pl.when((source >= 3) & has_after)
@@ -146,7 +149,7 @@
             remote(
                 halo_rows(a, j, source, 0, count, own),
                 kv_all.at[a, j, block(HALO + GROUP + source * ROWS, count), :],
-                z_send.at[1], halo_right.at[source // 2, j], (before, s),
+                z_send.at[1], halo_right.at[halo_index(j, source // 2)], (before, s),
             ).start()
 
         @pl.when((source <= 4) & has_before)
@@ -176,17 +179,17 @@
 
     def own_kv(a, j):
         return pltpu.make_async_copy(
-            source_of(a).at[:, cols(s * SLOTS + j)], kv_all.at[a, j, block(HALO + s * ROWS), :], own_sem.at[a]
+            source_of(a).at[:, cols(s * SLOTS + j)], kv_all.at[a, j, block(HALO + s * ROWS), :], own_sem.at[0]
         )
 
     def own_q(j):
         return pltpu.make_async_copy(
-            q_src.at[:, cols(s * SLOTS + j)], q_all.at[j, block(s * ROWS), :], own_sem.at[2]
+            q_src.at[:, cols(s * SLOTS + j)], q_all.at[j, block(s * ROWS), :], own_sem.at[1]
         )
 
     def own_out(j):
         return pltpu.make_async_copy(
-            o_buf.at[j, block(s * ROWS), :], out.at[:, cols(s * SLOTS + j)], own_sem.at[3]
+            o_buf.at[j, block(s * ROWS), :], out.at[:, cols(s * SLOTS + j)], own_sem.at[2]
         )
 
     def normalize(buf, gain, to):
@@ -201,11 +204,11 @@
         lax.fori_loop(0, SEQ * SLOTS // NORM_HEADS, some, 0)
 
     def wait_halo(sems, part, j, present):
-        count = 2 * min(2 * ROWS, HALO - part * 2 * ROWS)
+        count = 2 * min(2 * ROWS, HALO - part * 2 * ROWS) if j == SLOTS - 1 else 2 * HALO
 
         @pl.when(present)
         def _():
-            wait_all(kv_all.at[K, 0, pl.ds(0, count), :], sems.at[part, j])
+            wait_all(kv_all.at[K, 0, pl.ds(0, count), :], sems.at[halo_index(j, part)])
 
     def weigh(j, rows, keys):
         q = jnp.concatenate([q_all[j, rows, :], mark_q[rows, :]], axis=1)
@@ -229,9 +232,8 @@
 
     def attend_whole(j):
         wait_all(q_all.at[0, pl.ds(0, len(OTHERS) * ROWS), :], q_recv.at[j])
-        for part in range(PARTS):
-            wait_halo(halo_left, part, j, has_before)
-            wait_halo(halo_right, part, j, has_after)
+        wait_halo(halo_left, 0, j, has_before)
+        wait_halo(halo_right, 0, j, has_after)
         attend(j, 0, GROUP // BLOCK)
         for dx, dc in OTHERS:
             out_copy(j, partner(s, dx, dc), s).start()
@@ -401,17 +403,12 @@
 
     own_rows = block(s * ROWS)
     own_ext = block(HALO + s * ROWS)
-    wait_all(kv_all.at[K, :, own_ext, :], own_sem.at[0])
-    wait_all(kv_all.at[V, :, own_ext, :], own_sem.at[1])
-    wait_all(q_all.at[:, own_rows, :], own_sem.at[2])
+    wait_all(kv_all.at[:, :, own_ext, :], own_sem.at[0])
+    wait_all(q_all.at[:, own_rows, :], own_sem.at[1])
     for j in range(SLOTS - 1):
         attend_whole(j)
     attend_steps(SLOTS - 1)
 
-    sent = k_src.at[:, pl.ds(0, len(OTHERS) * SLOTS * HD)]
-    for i in range(3):
-        wait_all(sent, x_send.at[i])
-
     @pl.when(has_after)
     def _():
         wait_all(kv_all.at[:, :, pl.ds(0, HALO), :], z_send.at[0])
@@ -420,10 +417,9 @@
     def _():
         wait_all(kv_all.at[:, :, pl.ds(0, HALO), :], z_send.at[1])
 
-    wait_all(o_buf.at[:, own_rows, :], own_sem.at[3])
-    for j in range(SLOTS):
-        wait_all(out.at[:, pl.ds(0, len(OTHERS) * HD)], out_recv.at[j])
-    wait_all(sent, x_send.at[3])
+    wait_all(o_buf.at[:, own_rows, :], own_sem.at[2])
+    wait_all(out.at[:, pl.ds(0, len(OTHERS) * SLOTS * HD)], out_recv)
+    wait_all(kv_all.at[:, :, pl.ds(0, 2 * len(OTHERS) * ROWS), :], x_send)
 
 
 def solution(mesh):
@@ -457,16 +453,16 @@
                 pltpu.VMEM((1, SAMPLES), jnp.int32),
                 pltpu.VMEM((2, 8, HD), jnp.int32),
                 dma((6,)),
-                dma((4,)),
+                dma((3,)),
                 pltpu.SemaphoreType.REGULAR,
-                dma((4,)),
+                dma(()),
                 dma((2,)),
                 dma((SEQ,)),
                 dma((2, SLOTS)),
                 dma((SLOTS,)),
-                dma((PARTS, SLOTS)),
-                dma((PARTS, SLOTS)),
-                dma((SLOTS,)),
+                dma((SLOTS - 1 + PARTS,)),
+                dma((SLOTS - 1 + PARTS,)),
+                dma(()),
             ],
             compiler_params=pltpu.CompilerParams(
                 collective_id=0, has_side_effects=True, vmem_limit_bytes=VMEM_BYTES

time: 42.8 us -> 42.7 us (level)
  no operation moved by 1% of the time
where the time goes in v6:
time: 42.7 us; the launch traced here: 42.1 us
  Pallas kernels  41.2 us (96%)
  local copies, waits for them, and re-layouts  0.88 us (2%)
    pallas_call x1, Pallas kernels, local(): pl.pallas_call(functools.partial(kernel, groups), out_shape=jax.ShapeDtyp...  41.2 us
    unnamed x1, local copies, waits for them, and re-layouts  0.88 us

profile of v6, /device:TPU:1, one launch (start us, length us, event | category | flops | bytes accessed | tf_op | source)
XLA Modules:
  0.0 42.1 jit_solution(10144841063009843896)
XLA Ops:
  0.0 41.2 %joint_attention.1 = bf16[128,3072]{1,0:T(8,128)(2,1)S(1)} custom-call(bf16[128,3072]{1,0:T(8,128)(2,1)} %q_in.1, bf16[128,3072]{1,0:T(8,128)(2,1)} %k_in.1, bf16[128,3072]{1,0:T(8,128)(2,1)} %v_in.1, f32[1,128]{1,0:T(1,128)} %bitcast.4, f32[1,128]{1,0:T(1,128)} %bitcast.5, s32[1,64]{1,0:T(1,128)} %bitcast.6, s32[1,64]{1,0:T(1,128)} %bitcast.7), custom_call_target="tpu_custom_call" | custom-call | flops 4000000000 | bytes 4000000 | tf_op jit(solution)/shard_map/joint_attention/pallas_call | solution.py:436
  41.2 0.9 %copy.9 = bf16[128,3072]{1,0:T(8,128)(2,1)} copy(bf16[128,3072]{1,0:T(8,128)(2,1)S(1)} %joint_attention.1) | data formatting | bytes 1572864

commit v7 on v6

--- a/solution.py
+++ b/solution.py
@@ -243,7 +243,7 @@
         wait_all(q_all.at[0, pl.ds(0, len(OTHERS) * ROWS), :], q_recv.at[j])
         wait_halo(halo_left, 0, j, has_before)
         wait_halo(halo_right, 0, j, has_after)
-        left_late = (s < SEQ // 2) | ((s < 6) & (lax.rem(dp, 8) == 0) & has_before)
+        left_late = (s < SEQ // 2) | ((s < 5) & (lax.rem(dp, 8) == 0) & has_before)
         right_late = jnp.logical_not(left_late)
 
         def send_rows(first, count):

time: 42.7 us -> 42.7 us (level)
  no operation moved by 1% of the time
where the time goes in v7:
time: 42.7 us; the launch traced here: 42.1 us
  Pallas kernels  41.2 us (96%)
  local copies, waits for them, and re-layouts  0.88 us (2%)
    pallas_call x1, Pallas kernels, local(): pl.pallas_call(functools.partial(kernel, groups), out_shape=jax.ShapeDtyp...  41.2 us
    unnamed x1, local copies, waits for them, and re-layouts  0.88 us

profile of v7, /device:TPU:1, one launch (start us, length us, event | category | flops | bytes accessed | tf_op | source)
XLA Modules:
  0.0 42.1 jit_solution(5188608793541812184)
XLA Ops:
  0.0 41.2 %joint_attention.1 = bf16[128,3072]{1,0:T(8,128)(2,1)S(1)} custom-call(bf16[128,3072]{1,0:T(8,128)(2,1)} %q_in.1, bf16[128,3072]{1,0:T(8,128)(2,1)} %k_in.1, bf16[128,3072]{1,0:T(8,128)(2,1)} %v_in.1, f32[1,128]{1,0:T(1,128)} %bitcast.4, f32[1,128]{1,0:T(1,128)} %bitcast.5, s32[1,64]{1,0:T(1,128)} %bitcast.6, s32[1,64]{1,0:T(1,128)} %bitcast.7), custom_call_target="tpu_custom_call" | custom-call | flops 4000000000 | bytes 4000000 | tf_op jit(solution)/shard_map/joint_attention/pallas_call | solution.py:436
  41.2 0.9 %copy.9 = bf16[128,3072]{1,0:T(8,128)(2,1)} copy(bf16[128,3072]{1,0:T(8,128)(2,1)S(1)} %joint_attention.1) | data formatting | bytes 1572864
